TPU v7x, 32 devices: a whole 2x2x4 slice. The times are simulated.
32 devices in a mesh: facet: 8 (over z, core), row: 2 (over y), sub: 2 (over x).
Axes of the slice: x: 2, y: 2, z: 4, core: 2. Of those that a mesh axis runs over, the one named last changes fastest.
Arguments:
- facet_model: bfloat16 [2, 4, 8192, 8192], P(None, 'sub', ('facet', 'row')), may hold values from -6 to 6
- sub_offsets: int32 [32], replicated, may hold values from 0 to 65535
- tile_rows: int32 [32, 4], P(('facet', 'row', 'sub')), may hold values from 0 to 120
- tile_counts: int32 [32], P(('facet', 'row', 'sub')), may hold values from 1 to 4, as said below
- visibilities: bfloat16 [32, 4, 32, 8, 256], P(('facet', 'row', 'sub')), may hold values from -6 to 6
Outputs:
- residual_facets: bfloat16 [2, 4, 8192, 8192], P(None, 'sub', ('facet', 'row'))
- residual_vis: bfloat16 [32, 4, 32, 8, 256], P(('facet', 'row', 'sub'))
Inputs may be any that keep to these rules, and one draw needn't show every extreme that they name: tile_counts[s] tiles of subgrid s are live, the first ones; some subgrid has all 4 tiles live. Tile j of subgrid s covers subgrid rows tile_rows[s, j] to tile_rows[s, j] + 7; tiles may intersect.
All inputs are finite; a program needn't handle non-finite values.
Results may differ from a plain program's by a relative error of at most 0.014.
Values may be sent and summed in bfloat16 or wider, within the bound.
A program may use at most 192 MiB of HBM per device.

v0:
```python
import math

import jax
import jax.numpy as jnp
from jax import lax
from jax.sharding import PartitionSpec as P

SKY = 65536
CS = 64
SG = 128


two_pi = 2.0 * math.pi


def modmul(left, right, modulus):
    lower = right % 256
    upper = right // 256
    return (left * lower % modulus + left * upper % modulus * 256) % modulus


def window_taper(pixels):
    places = jnp.arange(pixels, dtype=jnp.float32)
    curve = jnp.sin(math.pi * (places + 0.5) / pixels)
    return 0.25 + 0.75 * curve * curve


def turn_pair(phase_index, modulus):
    angle = phase_index.astype(jnp.float32) * (-two_pi / modulus)
    return (jnp.cos(angle), jnp.sin(angle))


def column_table(facet_ids, pixels, width, modulus, ratio):
    spacing = modulus // pixels
    column_pos = facet_ids // ratio % ratio * pixels
    freqs = spacing * jnp.arange(width, dtype=jnp.int32)
    places = (column_pos[:, None] + jnp.arange(pixels, dtype=jnp.int32)[None, :]) % modulus
    cosine, sine = turn_pair(modmul(freqs[None, :, None], places[:, None, :], modulus), modulus)
    scaled = window_taper(pixels) / math.sqrt(pixels)
    return (jnp.stack([cosine, sine], axis=1) * scaled).astype(jnp.bfloat16)


def row_block(offsets, pixels, width, modulus, first_row, count):
    spacing = modulus // pixels
    freqs = (offsets[:, None] + spacing * jnp.arange(width, dtype=jnp.int32)[None, :]) % modulus
    places = first_row + jnp.arange(count, dtype=jnp.int32)
    cosine, sine = turn_pair(modmul(freqs[:, :, None], places[None, None, :], modulus), modulus)
    curve = jnp.sin(math.pi * (places.astype(jnp.float32) + 0.5) / pixels)
    scaled = (0.25 + 0.75 * curve * curve) / math.sqrt(pixels)
    return ((jnp.stack([cosine, sine], axis=1) * scaled).astype(jnp.bfloat16), freqs)


def facet_turn(freqs, facet_ids, modulus, pixels, ratio):
    row_pos = facet_ids % ratio * pixels
    return turn_pair(modmul(freqs[:, :, None], row_pos[None, None, :], modulus), modulus)


def grid_table(size):
    places = jnp.arange(size, dtype=jnp.int32)
    angle = (places[:, None] * places[None, :] % size).astype(jnp.float32) * (two_pi / size)
    return (jnp.stack([jnp.cos(angle), jnp.sin(angle)]) / math.sqrt(size)).astype(jnp.bfloat16)


def slot_table(count, ratio):
    facet_ids = jnp.arange(count, dtype=jnp.int32)
    first = facet_ids % ratio
    second = facet_ids // ratio % ratio
    options = jnp.arange(ratio, dtype=jnp.int32)
    hits = (first[:, None, None] == options[None, :, None]) & (
        second[:, None, None] == options[None, None, :]
    )
    return hits.astype(jnp.bfloat16)


def finish_contrib(raw, turn_real, turn_imag):
    part_real = raw[:, 0, :, :, :, 0] - raw[:, 1, :, :, :, 1]
    part_imag = raw[:, 0, :, :, :, 1] + raw[:, 1, :, :, :, 0]
    real_turn = turn_real[:, :, :, None, None]
    imag_turn = turn_imag[:, :, :, None, None]
    out_real = real_turn * part_real - imag_turn * part_imag
    out_imag = real_turn * part_imag + imag_turn * part_real
    joined = jnp.stack([out_real, out_imag], axis=4)
    return jnp.transpose(joined, (0, 2, 3, 1, 4, 5)).astype(jnp.bfloat16)


def assemble(contrib, slots, grid):
    width = contrib.shape[2]
    terms = contrib.shape[1]
    ratio = slots.shape[1]
    size = width * ratio
    placed = jnp.einsum("fab,ftkcl->katclb", slots, contrib, preferred_element_type=jnp.float32)
    amatrix = placed.reshape(size, terms, 2, size).astype(jnp.bfloat16)
    first = jnp.einsum("zum,mtcn->zutcn", grid, amatrix, preferred_element_type=jnp.float32)
    front = jnp.stack(
        [first[0, :, :, 0] - first[1, :, :, 1], first[0, :, :, 1] + first[1, :, :, 0]], axis=2
    ).astype(jnp.bfloat16)
    second = jnp.einsum("utcn,zvn->utczv", front, grid, preferred_element_type=jnp.float32)
    sky_real = second[:, :, 0, 0] - second[:, :, 1, 1]
    sky_imag = second[:, :, 0, 1] + second[:, :, 1, 0]
    return jnp.stack([sky_real, sky_imag], axis=2).astype(jnp.bfloat16)


def degrid_grid(sky_grid, rows, count, observed):
    slots_count, channels, tile_height, span = observed.shape
    size = sky_grid.shape[0]
    nu_values = (jnp.arange(channels, dtype=jnp.float32) + 0.5) / channels - 0.5
    live = jnp.arange(slots_count, dtype=jnp.int32) < count
    target = rows[:, None] + jnp.arange(tile_height, dtype=jnp.int32)[None, :]
    hits = (target[:, :, None] == jnp.arange(size, dtype=jnp.int32)[None, None, :]) & live[
        :, None, None
    ]
    placer = hits.astype(jnp.bfloat16).reshape(slots_count * tile_height, size)
    model_rows = jnp.dot(
        placer, sky_grid.reshape(size, 2 * span), preferred_element_type=jnp.float32
    )
    model_rows = model_rows.reshape(slots_count, tile_height, 2, span)
    model = model_rows[:, None, :, 0] + nu_values[None, :, None, None] * model_rows[:, None, :, 1]
    residual = (observed.astype(jnp.float32) - model) * live[:, None, None, None].astype(
        jnp.float32
    )
    weighted = jnp.stack(
        [jnp.sum(residual, axis=1), jnp.sum(nu_values[None, :, None, None] * residual, axis=1)],
        axis=2,
    )
    weighted = weighted.astype(jnp.bfloat16).reshape(slots_count * tile_height, 2 * span)
    regrid = lax.dot_general(
        placer, weighted, (((0,), (0,)), ((), ())), preferred_element_type=jnp.float32
    )
    return (residual.astype(jnp.bfloat16), regrid.reshape(size, 2, 2, size).astype(jnp.bfloat16))


def adjoint_grid(regrid, grid):
    first = jnp.einsum("zum,utcv->zmtcv", grid, regrid, preferred_element_type=jnp.float32)
    back_real = first[0, :, :, 0] + first[1, :, :, 1]
    back_imag = first[0, :, :, 1] - first[1, :, :, 0]
    back_front = jnp.stack([back_real, back_imag], axis=2).astype(jnp.bfloat16)
    second = jnp.einsum("mtcv,zvn->mtczn", back_front, grid, preferred_element_type=jnp.float32)
    grid_real = second[:, :, 0, 0] + second[:, :, 1, 1]
    grid_imag = second[:, :, 1, 0] - second[:, :, 0, 1]
    return jnp.stack([grid_real, grid_imag], axis=2).astype(jnp.bfloat16)


def select_slots(back_grid, slots):
    ratio = slots.shape[1]
    size = back_grid.shape[0]
    width = size // ratio
    terms = back_grid.shape[1]
    shaped = back_grid.reshape(width, ratio, terms, 2, width, ratio)
    return jnp.einsum(
        "fab,katclb->ftkcl", slots, shaped, preferred_element_type=jnp.float32
    ).astype(jnp.bfloat16)


def turn_back(returned, turn_real, turn_imag):
    real_turn = jnp.transpose(turn_real, (0, 2, 1))[:, :, None, :, None]
    imag_turn = jnp.transpose(turn_imag, (0, 2, 1))[:, :, None, :, None]
    part_real = returned[:, :, :, :, 0].astype(jnp.float32)
    part_imag = returned[:, :, :, :, 1].astype(jnp.float32)
    turned = jnp.stack(
        [
            real_turn * part_real + imag_turn * part_imag,
            real_turn * part_imag - imag_turn * part_real,
        ],
        axis=4,
    )
    return turned.astype(jnp.bfloat16)


def paired_terms(turned):
    real_part = turned[:, :, :, :, 0]
    imag_part = turned[:, :, :, :, 1]
    pair_real = jnp.stack([real_part, imag_part], axis=1)
    pair_imag = jnp.stack([imag_part, -real_part], axis=1)
    return jnp.stack([pair_real, pair_imag], axis=5)


def strip_terms(table_part, paired):
    return jnp.einsum("szkp,szftkcl->pftcl", table_part, paired, preferred_element_type=jnp.float32)


def local(facet_model, sub_offsets, tile_rows, tile_counts, visibilities):
    facets_here = facet_model.shape[1]
    rows_here = facet_model.shape[2]
    pixels = facet_model.shape[3]
    ratio = SG // CS
    pairs = lax.axis_size("sub")
    pair = lax.axis_index("sub")
    strip_group = lax.axis_index(("facet", "row"))
    facet_total = facets_here * pairs
    local_facets = pair * facets_here + jnp.arange(facets_here, dtype=jnp.int32)
    columns = column_table(local_facets, pixels, CS, SKY, ratio)
    strips = jnp.einsum(
        "tfpq,fckq->pftck", facet_model, columns, preferred_element_type=jnp.float32
    ).astype(jnp.bfloat16)
    group_offsets = lax.dynamic_slice_in_dim(sub_offsets, strip_group * pairs, pairs, 0)
    rtable, freqs = row_block(group_offsets, pixels, CS, SKY, 0, pixels)
    turn_real, turn_imag = facet_turn(freqs, local_facets, SKY, pixels, ratio)
    table_part = rtable
    raw = jnp.einsum(
        "szkp,pftcl->szkftcl",
        table_part,
        lax.all_gather(strips, ("facet", "row"), axis=0, tiled=True),
        preferred_element_type=jnp.float32,
    )
    contrib = finish_contrib(raw, turn_real, turn_imag)
    slots = slot_table(facet_total, ratio)
    grid = grid_table(SG)
    sky_grid = assemble(
        lax.all_to_all(contrib, "sub", split_axis=0, concat_axis=1, tiled=True)[0], slots, grid
    )
    residual, regrid = degrid_grid(sky_grid, tile_rows[0], tile_counts[0], visibilities[0])
    back_grid = adjoint_grid(regrid, grid)
    returned = select_slots(back_grid, slots)[None]
    received = lax.all_to_all(returned, "sub", split_axis=1, concat_axis=0, tiled=True)
    turned = turn_back(received, turn_real, turn_imag)
    first_row = strip_group * rows_here
    table_part, spare_freqs = row_block(sub_offsets, pixels, CS, SKY, first_row, rows_here)
    mine = strip_terms(
        table_part, paired_terms(lax.all_gather(turned, ("facet", "row"), axis=0, tiled=True))
    )
    strip_round = mine.astype(jnp.bfloat16)
    residual_facets = jnp.einsum(
        "pftck,fckq->tfpq", strip_round, columns, preferred_element_type=jnp.float32
    ).astype(jnp.bfloat16)
    return (residual_facets, residual[None])


def solution(mesh):
    placed = (
        P(None, "sub", ("facet", "row"), None),
        P(),
        P(("facet", "row", "sub"), None),
        P(("facet", "row", "sub")),
        P(("facet", "row", "sub"), None, None, None, None),
    )
    return jax.shard_map(
        local,
        mesh=mesh,
        in_specs=placed,
        out_specs=(
            P(None, "sub", ("facet", "row"), None),
            P(("facet", "row", "sub"), None, None, None, None),
        ),
        check_vma=False,
    )
```

profile of v0, /device:TPU:0, one launch (start us, length us, event | category | flops | bytes accessed | tf_op | source)
XLA Modules:
  0.0 330.4 jit_solution(11825774703770713795)
XLA Ops:
  7.2 0.1 fusion.121
  7.4 0.4 and_select_fusion.1
  7.8 21.4 %fusion.45 = (f32[2,1,64,8192]{3,2,1,0:T(8,128)}, f32[2,1,64,8192]{3,2,1,0:T(8,128)}) fusion(s32[2,8192]{1,0:T(2,128)S(1)} %get-tuple-element.41, s32[2,8192]{1,0:T(2,128)S(1)} %get-tuple-element.40, s32[64]{0:T(128)S(1)} %iota_multiply_fusion), kind=kLoop, calls=%fused_computation.90 | loop fusion | flops 40894464 | bytes 8519936 | tf_op jit(solution)/shard_map/cos | solution.py:30
  29.2 18.5 %fusion.63 = bf16[512,2,2,2,64]{0,4,3,2,1:T(8,128)(2,1)} fusion(f32[2,1,64,8192]{3,2,1,0:T(8,128)} %get-tuple-element.29, f32[2,1,64,8192]{3,2,1,0:T(8,128)} %get-tuple-element.28, f32[8192]{0:T(1024)S(1)} %fusion.121, bf16[2,2,512,8192]{3,2,1,0:T(8,128)(2,1)} %param.5), kind=kOutput, calls=%fused_computation.97 | convolution fusion | flops 4301520896 | bytes 42500096 | tf_op jit(solution)/shard_map/tfpq,fckq->pftck/dot_general | solution.py:192
  49.0 0.3 fusion.131
  49.3 0.1 fusion.181
  49.5 21.4 %fusion.43 = (f32[2,1,64,8192]{3,2,1,0:T(8,128)}, f32[2,1,64,8192]{3,2,1,0:T(8,128)}) fusion(s32[8192]{0:T(1024)S(1)} %get-tuple-element.48, s32[8192]{0:T(1024)S(1)} %get-tuple-element.49, s32[2,64]{1,0:T(2,128)S(1)} %and_select_fusion.15), kind=kLoop, calls=%fused_computation.88 | loop fusion | flops 40894464 | bytes 8454656 | tf_op jit(solution)/shard_map/cos | solution.py:30
  70.9 57.8 %all-gather.3.cloned.1.call-done = bf16[8192,2,2,2,64]{0,4,3,2,1:T(8,128)(2,1)} async-done(((bf16[512,2,2,2,64]{0,4,3,2,1:T(8,128)(2,1)}), bf16[8192,2,2,2,64]{0,4,3,2,1:T(8,128)(2,1)}) %all-gather.3.cloned.1.call-update) | async-done | bytes 8388624 | tf_op jit(solution)/shard_map/all_gather | solution.py:202
  128.7 8.2 %fusion.10 = f32[2,2,64,2,2,2,64]{6,2,5,4,3,1,0:T(8,128)S(1)} fusion(bf16[8192,2,2,2,64]{0,4,3,2,1:T(8,128)(2,1)} %all-gather.3.cloned.1.call-done, f32[2,1,64,8192]{3,2,1,0:T(8,128)} %get-tuple-element.31, f32[2,1,64,8192]{3,2,1,0:T(8,128)} %get-tuple-element.30, f32[8192]{0:T(1024)S(1)} %fusion.124), kind=kOutput, calls=%fused_computation.14 | convolution fusion | flops 2153775104 | bytes 17334272 | tf_op jit(solution)/shard_map/szkp,pftcl->szkftcl/dot_general | solution.py:199
  136.9 0.2 subtract_convert_fusion
  137.2 0.9 reshape.1387
  138.1 3.6 %all-to-all-start = ((bf16[2,2,16384]{2,1,0:T(2,128)(2,1)}), bf16[2,2,16384]{2,1,0:T(2,128)(2,1)S(1)}, u32[]{:S(2)}, u32[]{:S(2)}) async-start(bf16[2,2,16384]{2,1,0:T(2,128)(2,1)} %reshape.1387), calls=%async_computation | async-start | bytes 262144 | tf_op jit(solution)/shard_map/all_to_all | solution.py:209
  141.6 4.3 %all-to-all-done = bf16[2,2,16384]{2,1,0:T(2,128)(2,1)S(1)} async-done(((bf16[2,2,16384]{2,1,0:T(2,128)(2,1)}), bf16[2,2,16384]{2,1,0:T(2,128)(2,1)S(1)}, u32[]{:S(2)}, u32[]{:S(2)}) %all-to-all-start) | async-done | bytes 131104 | tf_op jit(solution)/shard_map/all_to_all | solution.py:209
  145.9 0.2 reshape.1388
  146.1 0.3 copy.115
  146.4 0.4 fusion.67
  146.8 6.4 %copy.116 = bf16[64,2,2,2,64,2]{5,4,1,0,3,2:T(8,128)(2,1)} copy(bf16[64,2,2,2,64,2]{4,5,1,3,0,2:T(2,128)(2,1)S(1)} %fusion.67) | data formatting | bytes 262144 | tf_op jit(solution)/shard_map/convert_element_type | solution.py:92
  153.2 13.1 %reshape.1374 = bf16[128,2,2,128,1]{3,0,2,1,4:T(8,128)(2,1)S(1)} reshape(bf16[64,2,2,2,64,2]{5,4,1,0,3,2:T(8,128)(2,1)} %copy.116) | data formatting | bytes 262144 | tf_op jit(solution)/shard_map/convert_element_type | solution.py:92
  166.3 0.2 fusion.112
  166.6 0.2 fusion.98
  166.9 0.2 fusion.140
  167.1 0.3 fusion.74
  167.5 0.5 fusion.75
  168.1 0.2 fusion.96
  168.3 10.0 %add.803 = bf16[64,2,2,1,64,2]{5,4,1,0,2,3:T(8,128)(2,1)} reshape(bf16[128,2,1,1,128]{4,0,3,2,1:T(8,128)(2,1)S(1)} %get-tuple-element.22) | data formatting | bytes 131072 | tf_op jit(solution)/shard_map/add | solution.py:138
  178.4 3.9 %copy.129 = bf16[64,2,2,1,64,2]{4,5,1,3,2,0:T(2,128)(2,1)S(1)} copy(bf16[64,2,2,1,64,2]{5,4,1,0,2,3:T(8,128)(2,1)} %add.803) | data formatting | bytes 131072 | tf_op jit(solution)/shard_map/add | solution.py:138
  182.2 10.0 %sub.147 = bf16[64,2,2,1,64,2]{5,4,1,0,2,3:T(8,128)(2,1)} reshape(bf16[128,2,1,1,128]{4,0,3,2,1:T(8,128)(2,1)S(1)} %get-tuple-element.23) | data formatting | bytes 131072 | tf_op jit(solution)/shard_map/sub | solution.py:139
  192.3 3.9 %copy.130 = bf16[64,2,2,1,64,2]{4,5,1,3,2,0:T(2,128)(2,1)S(1)} copy(bf16[64,2,2,1,64,2]{5,4,1,0,2,3:T(8,128)(2,1)} %sub.147) | data formatting | bytes 131072 | tf_op jit(solution)/shard_map/sub | solution.py:139
  196.1 0.5 fusion.68
  196.6 0.2 copy.190
  196.8 0.9 reshape.1389
  197.7 3.4 %all-to-all-start.1 = ((bf16[2,2,16384]{2,1,0:T(2,128)(2,1)}), bf16[2,2,16384]{2,1,0:T(2,128)(2,1)S(1)}, u32[]{:S(2)}, u32[]{:S(2)}) async-start(bf16[2,2,16384]{2,1,0:T(2,128)(2,1)} %reshape.1389), calls=%async_computation.1 | async-start | bytes 262144 | tf_op jit(solution)/shard_map/all_to_all | solution.py:214
  201.1 0.3 all-gather.5.cloned.1.call-start
  201.4 0.1 fusion.183
  201.5 4.0 %all-to-all-done.1 = bf16[2,2,16384]{2,1,0:T(2,128)(2,1)S(1)} async-done(((bf16[2,2,16384]{2,1,0:T(2,128)(2,1)}), bf16[2,2,16384]{2,1,0:T(2,128)(2,1)S(1)}, u32[]{:S(2)}, u32[]{:S(2)}) %all-to-all-start.1) | async-done | bytes 131104 | tf_op jit(solution)/shard_map/all_to_all | solution.py:214
  205.6 0.2 reshape.1390
  206.3 0.8 pad_maximum_fusion.2
  207.2 22.1 %fusion.41 = (f32[32,1,64,512]{3,2,1,0:T(8,128)}, f32[32,1,64,512]{3,2,1,0:T(8,128)}) fusion(s32[512]{0:T(512)S(1)} %get-tuple-element.52, s32[512]{0:T(512)S(1)} %get-tuple-element.53, s32[32,64]{1,0:T(8,128)S(1)} %add_select_fusion.13), kind=kLoop, calls=%fused_computation.86 | loop fusion | flops 40894464 | bytes 8400896 | tf_op jit(solution)/shard_map/cos | solution.py:30
  229.4 1.2 fusion.73
  230.5 25.0 %all-gather.5.cloned.1.call-done = bf16[32,2,2,64,2,64]{3,5,0,2,1,4:T(8,128)(2,1)} async-done(((bf16[2,2,2,64,2,64]{3,5,0,2,1,4:T(8,128)(2,1)}), bf16[32,2,2,64,2,64]{3,5,0,2,1,4:T(8,128)(2,1)}) %all-gather.5.cloned.1.call-update) | async-done | bytes 2097168 | tf_op jit(solution)/shard_map/all_gather | solution.py:219
  255.5 3.4 %slice_bitcast_fusion.1 = (bf16[32,1,2,2,64,64]{4,5,1,0,3,2:T(8,128)(2,1)S(1)}, bf16[32,1,2,2,64,64]{4,5,1,0,3,2:T(8,128)(2,1)S(1)}) fusion(bf16[32,2,2,64,2,64]{3,5,0,2,1,4:T(8,128)(2,1)} %all-gather.5.cloned.1.call-done), kind=kLoop, calls=%fused_computation.84 | loop fusion | bytes 4194304 | tf_op jit(solution)/shard_map/stack;squeeze | solution.py:172
  258.9 0.3 fusion.192
  259.2 1.3 maximum_bitcast_fusion
  260.5 0.9 copy-done.1
  261.4 1.3 copy-done.2
  262.7 2.9 fusion.51.clone.5
  265.5 17.4 %fusion = bf16[2,2,512,8192]{2,3,0,1:T(8,128)(2,1)} fusion(f32[2,1,64,8192]{3,2,1,0:T(8,128)} %get-tuple-element.29, f32[2,1,64,8192]{3,2,1,0:T(8,128)} %get-tuple-element.28, f32[8192]{0:T(1024)S(1)} %fusion.121, bf16[512,2,2,2,64]{0,4,3,2,1:T(8,128)(2,1)S(1)} %fusion.51.clone.5), kind=kOutput, calls=%fused_computation.1 | convolution fusion | flops 4318035968 | bytes 42500096 | tf_op jit(solution)/shard_map/pftck,fckq->tfpq/dot_general | solution.py:222
  283.0 40.6 %copy.136 = bf16[2,2,512,8192]{3,2,1,0:T(8,128)(2,1)} copy(bf16[2,2,512,8192]{2,3,0,1:T(8,128)(2,1)} %fusion) | data formatting | bytes 67108864
  (53 shorter events, 1.7 us)
Async XLA Ops:
  7.2 121.5 %all-gather.3.cloned.1.call-start = ((), (), s32[]{:S(2)}) async-start(), calls=%async_computation.2 | async-start | bytes 8912896 | tf_op jit(solution)/shard_map/all_gather | solution.py:202
  29.2 19.4 %copy-start.4 = (s32[1,4]{1,0:T(1,128)S(1)}, s32[1,4]{1,0:T(1,128)}, u32[]{:S(2)}) copy-start(s32[1,4]{1,0:T(1,128)} %param.7) | copy-start | bytes 52
  29.2 19.5 %copy-start.5 = (s32[32]{0:T(128)S(1)}, s32[32]{0:T(128)}, u32[]{:S(2)}) copy-start(s32[32]{0:T(128)} %param.6) | copy-start | bytes 388
  138.1 7.8 %all-to-all-start = ((bf16[2,2,16384]{2,1,0:T(2,128)(2,1)}), bf16[2,2,16384]{2,1,0:T(2,128)(2,1)S(1)}, u32[]{:S(2)}, u32[]{:S(2)}) async-start(bf16[2,2,16384]{2,1,0:T(2,128)(2,1)} %reshape.1387), calls=%async_computation | async-start | bytes 262144 | tf_op jit(solution)/shard_map/all_to_all | solution.py:209
  153.2 13.9 %copy-start.3 = (bf16[1,4,32,8,256]{4,3,2,1,0:T(8,128)(2,1)S(1)}, bf16[1,4,32,8,256]{4,3,2,1,0:T(8,128)(2,1)}, u32[]{:S(2)}) copy-start(bf16[1,4,32,8,256]{4,3,2,1,0:T(8,128)(2,1)} %param.9) | copy-start | bytes 1572868
  197.7 7.8 %all-to-all-start.1 = ((bf16[2,2,16384]{2,1,0:T(2,128)(2,1)}), bf16[2,2,16384]{2,1,0:T(2,128)(2,1)S(1)}, u32[]{:S(2)}, u32[]{:S(2)}) async-start(bf16[2,2,16384]{2,1,0:T(2,128)(2,1)} %reshape.1389), calls=%async_computation.1 | async-start | bytes 262144 | tf_op jit(solution)/shard_map/all_to_all | solution.py:214
  201.1 54.3 %all-gather.5.cloned.1.call-start = ((), (), s32[]{:S(2)}) async-start(), calls=%async_computation.3 | async-start | bytes 4456448 | tf_op jit(solution)/shard_map/all_gather | solution.py:219
  255.5 3.4 %copy-start = (bf16[32,2,2,64,2,64]{3,5,0,2,1,4:T(8,128)(2,1)S(1)}, bf16[32,2,2,64,2,64]{3,5,0,2,1,4:T(8,128)(2,1)}, u32[]{:S(2)}) copy-start(bf16[32,2,2,64,2,64]{3,5,0,2,1,4:T(8,128)(2,1)} %all-gather.5.cloned.1.call-done) | copy-start | bytes 6291460
  259.2 2.2 copy-start.1
  259.2 3.5 %copy-start.2 = (f32[32,1,64,512]{3,2,1,0:T(8,128)S(1)}, f32[32,1,64,512]{3,2,1,0:T(8,128)}, u32[]{:S(2)}) copy-start(f32[32,1,64,512]{3,2,1,0:T(8,128)} %get-tuple-element.35) | copy-start | bytes 12582916
Sparse Core Ops, SparseCore 0:
  47.8 80.8 all-gather.2
  207.2 48.2 all-gather.4
where the time goes:
time: 332 us; the launch traced here: 330 us
  local copies, waits for them, and re-layouts  96.9 us (29%)
  waiting for transfers between devices  91.1 us (27%)
  other arithmetic  70.8 us (21%)
  matrix products  49.2 us (15%)
  between operations  15.1 us (5%)
  starting transfers between devices  7.24 us (2%)
    cos x5, other arithmetic, turn_pair(): return (jnp.cos(angle), jnp.sin(angle))  65.2 us
    all_gather x1, waiting for transfers between devices, local(): lax.all_gather(strips, ('facet', 'row'), axis=0, tiled=True)  57.8 us
    unnamed x20, local copies, waits for them, and re-layouts  45.3 us
    all_gather x1, waiting for transfers between devices, local(): lax.all_gather(turned, ('facet', 'row'), axis=0, tiled=True)  25 us
    convert_element_type x2, local copies, waits for them, and re-layouts, assemble(): amatrix = placed.reshape(size, terms, 2, size).astype(jnp.bfloat16)  19.5 us
    dot_general x1, matrix products, local(): jnp.einsum('tfpq,fckq->pftck', facet_model, columns, preferred_element_ty...  18.5 us
    dot_general x1, matrix products, local(): jnp.einsum('pftck,fckq->tfpq', strip_round, columns, preferred_element_ty...  17.4 us
    sub x2, local copies, waits for them, and re-layouts, adjoint_grid(): grid_imag = second[:, :, 1, 0] - second[:, :, 0, 1]  13.9 us
  transfers between devices with their start and end apart: 4, of which 4 were waited for; matrix products, arithmetic and copies ran while one was open for 14% of the time, Pallas kernels for 0%

commit v1 on v0

v1 whole, which is shorter than its diff:
```python
import functools
import math

import jax
import jax.numpy as jnp
from jax import lax
from jax.experimental import pallas as pl
from jax.experimental.pallas import tpu as pltpu
from jax.sharding import PartitionSpec as P

SKY = 65536
CS = 64
SG = 128
TERMS = 2

two_pi = 2.0 * math.pi
F32 = jnp.float32
BF16 = jnp.bfloat16


def unit(phase, modulus, sign=-1.0):
    angle = phase.astype(F32) * (sign * two_pi / modulus)
    return jnp.cos(angle), jnp.sin(angle)


def taper_of(places, pixels):
    curve = jnp.sin(math.pi * (places.astype(F32) + 0.5) / pixels)
    return (0.25 + 0.75 * curve * curve) / math.sqrt(pixels)


def iota(count):
    return jnp.arange(count, dtype=jnp.int32)


def column_table(pixels):
    spacing = SKY // pixels
    freqs = spacing * iota(CS)
    lane = 128
    low = unit(freqs[:, None] * iota(lane)[None, :] % SKY, SKY)
    high = unit(freqs[:, None] * (lane * iota(pixels // lane))[None, :] % SKY, SKY)
    scale = taper_of(iota(pixels), pixels).reshape(pixels // lane, lane)
    lr, li, hr, hi, scale = lax.optimization_barrier((*low, *high, scale))
    lr, li, hr, hi = lr[:, None, :], li[:, None, :], hr[:, :, None], hi[:, :, None]
    real = (hr * lr - hi * li) * scale
    imag = (hr * li + hi * lr) * scale
    return jnp.concatenate([real, imag], axis=0).astype(BF16).reshape(2 * CS, pixels)


def row_table(offsets, pixels, first_row, count):
    spacing = SKY // pixels
    places = first_row + iota(count)
    base = unit(offsets[:, None] * places[None, :] % SKY, SKY)
    step = unit(spacing * iota(CS)[:, None] * places[None, :] % SKY, SKY)
    scale = taper_of(places, pixels)
    br, bi, sr, si = lax.optimization_barrier((*base, step[0] * scale, step[1] * scale))
    br, bi, sr, si = br[:, None, :], bi[:, None, :], sr[None], si[None]
    real = br * sr - bi * si
    imag = br * si + bi * sr
    return real.astype(BF16), imag.astype(BF16)


def grid_tables():
    ratio = SG // CS
    order = (ratio * iota(CS)[None, :] + iota(ratio)[:, None]).reshape(SG)
    cosine, sine = unit(iota(SG)[:, None] * order[None, :] % SG, SG, 1.0)
    real = (cosine / math.sqrt(SG)).astype(BF16)
    imag = (sine / math.sqrt(SG)).astype(BF16)
    left = jnp.concatenate([real, imag], axis=1)
    back = jnp.concatenate([real.T, imag.T], axis=1)
    tr = real.T.reshape(ratio, CS, SG)
    ti = imag.T.reshape(ratio, CS, SG)
    right = jnp.stack(
        [jnp.concatenate([tr, ti], axis=2), jnp.concatenate([-ti, tr], axis=2)], axis=1
    ).reshape(2 * SG, 2 * SG)
    return left, back, right, right.T


def times_i(value):
    half = value.shape[-1] // 2
    return jnp.concatenate([-value[..., half:], value[..., :half]], axis=-1)


def dot(left, right):
    return jnp.dot(left, right, preferred_element_type=F32)


def subgrid_cycle(offset_mod, spacing, rows, count, contrib, left, back, right, right_t, observe, emit):
    ratio = SG // CS
    slot = lax.broadcasted_iota(jnp.int32, (SG, 1), 0) // CS
    angle = (offset_mod * slot % spacing).astype(F32) * (-two_pi / spacing)
    turn_r, turn_i = jnp.cos(angle), jnp.sin(angle)
    fronts = []
    for t in range(TERMS):
        parts = []
        for b in range(ratio):
            raw = contrib(t, b)
            placed = (turn_r * raw + turn_i * times_i(raw)).astype(BF16)
            parts.append(jnp.concatenate([placed, times_i(placed)], axis=0))
        fronts.append(dot(left, jnp.concatenate(parts, axis=1)).astype(BF16))
    sky = [dot(front, right).astype(BF16) for front in fronts]
    tiles = len(rows)
    height = 8
    group = tiles * height
    line = lax.broadcasted_iota(jnp.int32, (group, 1), 0)
    target = jnp.zeros((group, 1), jnp.int32)
    for j in range(tiles):
        target = jnp.where(line // height == j, rows[j] + line - j * height, target)
    live = line // height < count
    column = lax.broadcasted_iota(jnp.int32, (group, SG), 1)
    placer = jnp.where((target == column) & live, 1.0, 0.0).astype(BF16)
    model = [dot(placer, term) for term in sky]
    live_f = live.astype(F32)
    sums = [[], []]
    for j in range(tiles):
        part = slice(j * height, (j + 1) * height)
        sums_j = observe(j, model[0][part], model[1][part], live_f[part])
        sums[0].append(sums_j[0])
        sums[1].append(sums_j[1])
    out = []
    for t in range(TERMS):
        weighted = jnp.concatenate(sums[t], axis=0).astype(BF16)
        regrid = lax.dot_general(
            placer, weighted, (((0,), (0,)), ((), ())), preferred_element_type=F32
        ).astype(BF16)
        front = dot(back, jnp.concatenate([regrid, -times_i(regrid)], axis=0)).astype(BF16)
        grid = dot(front, right_t).astype(BF16).astype(F32)
        out.append([])
        for b in range(ratio):
            part = grid[:, b * SG : (b + 1) * SG]
            out[t].append((turn_r * part - turn_i * times_i(part)).astype(BF16))
    return out


def observe_tile(vis_ref, res_ref, j, first, second, live):
    channels = vis_ref.shape[1]
    sum0 = jnp.zeros(first.shape, F32)
    sum1 = jnp.zeros(first.shape, F32)
    for c in range(channels):
        nu = (c + 0.5) / channels - 0.5
        residual = (vis_ref[j, c].astype(F32) - (first + nu * second)) * live
        res_ref[j, c] = residual.astype(BF16)
        sum0 += residual
        sum1 += nu * residual
    return sum0, sum1


def cycle_kernel(spacing, scal_ref, x_ref, left_ref, back_ref, right_ref, right_t_ref, vis_ref, y_ref, res_ref):
    tiles = vis_ref.shape[0]
    rows = [scal_ref[2 + j] for j in range(tiles)]
    out = subgrid_cycle(
        scal_ref[0], spacing, rows, scal_ref[1],
        lambda t, b: x_ref[t, b].astype(F32),
        left_ref[...], back_ref[...], right_ref[...], right_t_ref[...],
        functools.partial(observe_tile, vis_ref, res_ref), None,
    )
    for t in range(TERMS):
        for b in range(SG // CS):
            y_ref[t, b] = out[t][b]


def local(facet_model, sub_offsets, tile_rows, tile_counts, visibilities):
    terms, facets, rows_here, pixels = facet_model.shape
    spacing = SKY // pixels
    ratio = SG // CS
    pairs = lax.axis_size("sub")
    pair = lax.axis_index("sub")
    strip_group = lax.axis_index(("facet", "row"))
    owner = strip_group * pairs + pair
    columns = column_table(pixels)
    real, imag = row_table(sub_offsets, pixels, strip_group * rows_here, rows_here)
    table = jnp.stack([real, imag], axis=2)
    strips = jnp.einsum(
        "tfpq,nq->tfpn", facet_model, columns, preferred_element_type=F32
    ).astype(BF16)
    both = jnp.stack([strips, times_i(strips)], axis=2)
    partial = jnp.einsum("skzp,tfzpn->tfskn", table, both, preferred_element_type=F32).astype(BF16)
    summed = lax.psum_scatter(partial, ("facet", "row"), scatter_dimension=2, tiled=True)
    contrib = lax.all_to_all(summed, "sub", split_axis=2, concat_axis=1, tiled=True)
    contrib = contrib.reshape(terms, ratio, SG, 2 * CS)
    left, back, right, right_t = grid_tables()
    scal = jnp.concatenate(
        [lax.dynamic_slice(sub_offsets, (owner,), (1,)) % spacing, tile_counts, tile_rows[0]]
    )
    vmem = pl.BlockSpec(memory_space=pltpu.VMEM)
    returned, residual = pl.pallas_call(
        functools.partial(cycle_kernel, spacing),
        out_shape=(
            jax.ShapeDtypeStruct(contrib.shape, BF16),
            jax.ShapeDtypeStruct(visibilities.shape[1:], BF16),
        ),
        in_specs=[pl.BlockSpec(memory_space=pltpu.SMEM)] + [vmem] * 6,
        out_specs=(vmem, vmem),
        compiler_params=pltpu.CompilerParams(vmem_limit_bytes=32 * 2**20),
    )(scal, contrib, left, back, right, right_t, visibilities[0])
    returned = returned.reshape(terms, facets * pairs, 1, CS, 2 * CS)
    received = lax.all_to_all(returned, "sub", split_axis=1, concat_axis=2, tiled=True)
    turned = lax.all_gather(received, ("facet", "row"), axis=2, tiled=True)
    pairs_of = jnp.stack([turned, -times_i(turned)], axis=4)
    strip_round = jnp.einsum(
        "skzp,tfskzn->tfpn", table, pairs_of, preferred_element_type=F32
    ).astype(BF16)
    residual_facets = jnp.einsum(
        "tfpn,nq->tfpq", strip_round, columns, preferred_element_type=F32
    ).astype(BF16)
    return (residual_facets, residual[None])


def solution(mesh):
    placed = (
        P(None, "sub", ("facet", "row"), None),
        P(),
        P(("facet", "row", "sub"), None),
        P(("facet", "row", "sub")),
        P(("facet", "row", "sub"), None, None, None, None),
    )
    return jax.shard_map(
        local,
        mesh=mesh,
        in_specs=placed,
        out_specs=(
            P(None, "sub", ("facet", "row"), None),
            P(("facet", "row", "sub"), None, None, None, None),
        ),
        check_vma=False,
    )
```

time: 332 us -> 227 us (0.68)
  local copies, waits for them, and re-layouts: 96.9 us -> 7.74 us
  other arithmetic: 70.8 us -> 14 us
  waiting for transfers between devices: 91.1 us -> 138 us
  matrix products: 49.2 us -> 36.6 us
  blocking collectives: 0 us -> 6.85 us
  starting transfers between devices: 7.24 us -> 3.46 us
    unnamed x2 -> x3, waiting for transfers between devices: 0.03 us -> 94.1 us
    cos x5 -> x0, other arithmetic: 65.2 us -> none  [turn_pair(): return (jnp.cos(angle), jnp.sin(angle))]
    all_gather x2 -> x1, waiting for transfers between devices: 82.8 us -> 39.9 us  [local(): turned = lax.all_gather(received, ('facet', 'row'), axis=2, tiled=True)]
    unnamed x20, local copies, waits for them, and re-layouts: 45.3 us -> 5.62 us
    convert_element_type x2 -> x0, local copies, waits for them, and re-layouts: 19.5 us -> none  [assemble(): amatrix = placed.reshape(size, terms, 2, size).astype(jnp.bfloat16)]
    add x4 -> x1, local copies, waits for them, and re-layouts: 14 us -> 0.08 us  [grid_tables(): order = (ratio * iota(CS)[None, :] + iota(ratio)[:, None]).reshape(SG)]
    sub x2 -> x0, local copies, waits for them, and re-layouts: 13.9 us -> none  [adjoint_grid(): grid_imag = second[:, :, 1, 0] - second[:, :, 0, 1]]
    dot_general x11 -> x4, matrix products: 49.2 us -> 36.6 us  [the longest x1 16.2 us: local(): jnp.einsum('tfpq,nq->tfpn', facet_model, columns, preferred_element_type=...]
  transfers between devices with their start and end apart: 4 -> 3, of which waited for: 4 -> 3; matrix products, arithmetic and copies ran while one was open for 14% -> 1% of each run, Pallas kernels for 0% -> 0%
where the time goes in v1:
time: 227 us
  waiting for transfers between devices  138 us (61%)
  matrix products  36.6 us (16%)
  between operations  17.6 us (8%)
  other arithmetic  14 us (6%)
  local copies, waits for them, and re-layouts  7.74 us (3%)
  blocking collectives  6.85 us (3%)
  starting transfers between devices  3.46 us (2%)
  Pallas kernels  2.38 us (1%)
    unnamed x3, waiting for transfers between devices  94.1 us
    all_gather x1, waiting for transfers between devices, local(): turned = lax.all_gather(received, ('facet', 'row'), axis=2, tiled=True)  39.9 us
    dot_general x1, matrix products, local(): jnp.einsum('tfpq,nq->tfpn', facet_model, columns, preferred_element_type=...  16.2 us
    dot_general x1, matrix products, local(): jnp.einsum('tfpn,nq->tfpq', strip_round, columns, preferred_element_type=...  14.3 us
    all_to_all x1, blocking collectives, local(): lax.all_to_all(returned, 'sub', split_axis=1, concat_axis=2, tiled=True)  6.85 us
    unnamed x20, local copies, waits for them, and re-layouts  5.62 us
  transfers between devices with their start and end apart: 3, of which 3 were waited for; matrix products, arithmetic and copies ran while one was open for 1% of the time, Pallas kernels for 0%

profile of v1, /device:TPU:0, one launch (start us, length us, event | category | flops | bytes accessed | tf_op | source)
XLA Modules:
  0.0 226.9 jit_solution(2310646606469334992)
XLA Ops:
  7.2 0.0 all-reduce.3.cloned.1.call-start
  7.2 0.1 fusion.55
  7.3 0.1 fusion.42
  7.4 0.2 fusion.51
  7.7 0.2 fusion.49
  7.9 1.0 fusion.44
  8.9 0.6 sine_multiply_fusion
  9.5 1.1 multiply_subtract_fusion
  10.6 3.4 %fusion.4 = (bf16[64,8192]{1,0:T(8,128)(2,1)S(1)}, bf16[64,8192]{1,0:T(8,128)(2,1)S(1)}) fusion(f32[8,8,64,128]{3,2,1,0:T(8,128)S(1)} %bitcast.91, f32[8192]{0:T(1024)S(1)} %bitcast.98, f32[8,8,64,128]{3,2,1,0:T(8,128)S(1)} %bitcast.92), kind=kLoop, calls=%fused_computation.12 | loop fusion | flops 2097152 | bytes 6324224 | tf_op jit(solution)/shard_map/convert
  14.0 16.2 %fusion.8 = bf16[128,2,2,512]{3,0,2,1:T(8,128)(2,1)S(1)} fusion(bf16[2,2,512,8192]{3,2,1,0:T(8,128)(2,1)} %param.5, bf16[64,8192]{1,0:T(8,128)(2,1)S(1)} %get-tuple-element.35, bf16[64,8192]{1,0:T(8,128)(2,1)S(1)} %get-tuple-element.34), kind=kOutput, calls=%fused_computation.22 | convolution fusion | flops 4299423744 | bytes 36175872 | tf_op jit(solution)/shard_map/tfpq,nq->tfpn/dot_general | solution.py:172
  30.4 1.4 subtract_convert_fusion
  31.8 0.0 copy-start.2
  31.8 0.0 copy-start.4
  31.8 1.3 copy-done.2
  33.1 0.7 copy-done.4
  33.8 3.7 %fusion.6 = bf16[2,2,32,64,128]{4,3,2,1,0:T(8,128)(2,1)} fusion(bf16[32,64,1,512]{3,1,2,0:T(8,128)(2,1)S(1)} %get-tuple-element.29, bf16[32,64,1,512]{3,1,2,0:T(8,128)(2,1)S(1)} %get-tuple-element.28, bf16[2,2,1,512,128]{3,4,1,0,2:T(8,128)(2,1)S(1)} %maximum_bitcast_fusion.7, bf16[2,2,1,512,128]{3,4,1,0,2:T(8,128)(2,1)S(1)} %bitcast.90), kind=kOutput, calls=%fused_computation.20 | convolution fusion | flops 2157445120 | bytes 7340032 | tf_op jit(solution)/shard_map/skzp,tfzpn->tfskn/dot_general | solution.py:176
  37.4 0.0 all-reduce.3.cloned.1.call-update
  37.5 0.6 copy-done.6
  38.1 0.6 dynamic_slice.3
  41.3 0.1 add.227
  41.4 0.3 fusion.53
  41.7 0.3 multiply_convert_fusion
  42.1 0.1 copy.27
  42.2 0.0 copy-done.8
  42.2 0.6 dynamic-slice
  43.5 0.6 multiply_convert_fusion.3
  44.1 94.1 %all-reduce.3.cloned.1.call-done = bf16[2,2,32,64,128]{4,3,2,1,0:T(8,128)(2,1)} async-done(((bf16[2,2,32,64,128]{4,3,2,1,0:T(8,128)(2,1)}), bf16[2,2,32,64,128]{4,3,2,1,0:T(8,128)(2,1)}) %all-reduce.3.cloned.1.call-update) | async-done | bytes 2097168
  138.1 0.9 constant_dynamic-slice_fusion
  139.0 0.7 copy.24
  139.7 3.4 %all-to-all-start = ((bf16[2,2,2,64,128]{4,3,1,0,2:T(8,128)(2,1)}), bf16[2,2,2,64,128]{4,3,1,0,2:T(8,128)(2,1)S(1)}, u32[]{:S(2)}, u32[]{:S(2)}) async-start(bf16[2,2,2,64,128]{4,3,1,0,2:T(8,128)(2,1)} %copy.24), calls=%async_computation | async-start | bytes 262144 | tf_op jit(solution)/shard_map/all_to_all | solution.py:178
  143.1 0.0 all-gather.3.cloned.1.call-start
  143.1 0.0 copy-done.7
  143.2 0.1 pad_add_fusion.scal_ref
  143.2 4.3 %all-to-all-done = bf16[2,2,2,64,128]{4,3,1,0,2:T(8,128)(2,1)S(1)} async-done(((bf16[2,2,2,64,128]{4,3,1,0,2:T(8,128)(2,1)}), bf16[2,2,2,64,128]{4,3,1,0,2:T(8,128)(2,1)S(1)}, u32[]{:S(2)}, u32[]{:S(2)}) %all-to-all-start) | async-done | bytes 131104 | tf_op jit(solution)/shard_map/all_to_all | solution.py:178
  147.6 0.0 copy-done
  147.6 2.4 %shard_map.68 = (bf16[2,2,128,128]{3,2,1,0:T(8,128)(2,1)S(1)}, bf16[4,32,8,256]{3,2,1,0:T(8,128)(2,1)}) custom-call(s32[6]{0:T(128)S(1)} %pad_add_fusion.scal_ref, bf16[2,2,128,128]{3,2,1,0:T(8,128)(2,1)S(1)} %bitcast.87, bf16[128,256]{1,0:T(8,128)(2,1)S(1)} %get-tuple-element.52.left_ref, bf16[128,256]{1,0:T(8,128)(2,1)S(1)} %get-tuple-element.53.back_ref, ...), custom_call_target="tpu_custom_call" | custom-call | tf_op jit(solution)/shard_map/pallas_call | solution.py:185
  150.0 6.8 %all_to_all.33 = bf16[2,4,1,64,128]{4,3,0,2,1:T(8,128)(2,1)S(1)} all-to-all(bf16[2,4,1,64,128]{4,3,0,2,1:T(8,128)(2,1)S(1)} %copy.28), channel_id=1, replica_groups=mesh['facet'=8,'row'=2,'sub'=2] {'sub'}, dimensions={1} | all-to-all | bytes 262144 | tf_op jit(solution)/shard_map/all_to_all | solution.py:196
  156.8 0.7 copy.64
  157.5 0.0 all-gather.3.cloned.1.call-update
  157.5 39.9 %all-gather.3.cloned.1.call-done = bf16[2,2,32,1,64,128]{5,4,2,1,0,3:T(8,128)(2,1)} async-done(((bf16[2,2,2,1,64,128]{5,4,2,1,0,3:T(8,128)(2,1)}), bf16[2,2,32,1,64,128]{5,4,2,1,0,3:T(8,128)(2,1)}) %all-gather.3.cloned.1.call-update) | async-done | bytes 2097168 | tf_op jit(solution)/shard_map/all_gather | solution.py:197
  197.5 3.1 %fusion.5 = (bf16[2,2,32,64,1,64]{5,3,2,1,0,4:T(8,128)(2,1)S(1)}, bf16[2,2,32,64,1,64]{5,3,2,1,0,4:T(8,128)(2,1)S(1)}) fusion(bf16[2,2,32,64,128]{4,3,2,1,0:T(8,128)(2,1)} %bitcast.93), kind=kLoop, calls=%fused_computation.15 | loop fusion | flops 524288 | bytes 4194304 | tf_op jit(solution)/shard_map/concatenate | solution.py:80
  200.6 0.0 copy-start.5
  200.6 1.3 maximum_negate_fusion
  201.9 0.3 copy-done.1
  202.1 0.6 copy-done.3
  202.8 0.6 copy-done.5
  203.4 2.4 %fusion = bf16[2,2,128,512,1,1]{3,2,4,0,1,5:T(8,128)(2,1)S(1)} fusion(bf16[32,64,1,512]{3,1,2,0:T(8,128)(2,1)S(1)} %copy-done.5, bf16[32,64,1,512]{3,1,2,0:T(8,128)(2,1)S(1)} %copy-done.3, bf16[2,2,32,64,1,128]{5,3,2,1,0,4:T(8,128)(2,1)S(1)} %maximum_negate_fusion, bf16[2,2,32,64,1,128]{5,3,2,1,0,4:T(8,128)(2,1)S(1)} %bitcast.94), kind=kOutput, calls=%fused_computation.3 | convolution fusion | flops 2151677952 | bytes 8912896 | tf_op jit(solution)/shard_map/skzp,tfskzn->tfpn/dot_general | solution.py:199
  205.8 14.3 %convolution_convert_fusion = bf16[2,2,512,8192]{3,2,1,0:T(8,128)(2,1)} fusion(bf16[64,8192]{1,0:T(8,128)(2,1)S(1)} %get-tuple-element.35, bf16[64,8192]{1,0:T(8,128)(2,1)S(1)} %get-tuple-element.34, bf16[2,2,128,512,1,1]{3,2,4,0,1,5:T(8,128)(2,1)S(1)} %fusion), kind=kOutput, calls=%fused_computation | convolution fusion | flops 4315938816 | bytes 36175872 | tf_op jit(solution)/shard_map/tfpn,nq->tfpq/dot_general | solution.py:202
  (18 shorter events, 0.2 us)
Async XLA Ops:
  7.2 131.0 %all-reduce.3.cloned.1.call-start = ((), (), s32[]{:S(2)}) async-start(), calls=%async_computation.3 | async-start | bytes 4194304
  31.8 1.3 copy-start.2
  31.8 2.0 copy-start.4
  37.4 0.7 copy-start.6
  37.4 4.8 %copy-start.8 = (u32[32]{0:T(128)S(1)}, u32[32]{0:T(128)}, u32[]{:S(2)}) copy-start(u32[32]{0:T(128)} %constant.140) | copy-start | bytes 388
  37.4 105.7 %copy-start.7 = (s32[1,4]{1,0:T(1,128)S(1)}, s32[1,4]{1,0:T(1,128)}, u32[]{:S(2)}) copy-start(s32[1,4]{1,0:T(1,128)} %param.7) | copy-start | bytes 52
  37.4 110.1 %copy-start = (bf16[1,4,32,8,256]{4,3,2,1,0:T(8,128)(2,1)S(1)}, bf16[1,4,32,8,256]{4,3,2,1,0:T(8,128)(2,1)}, u32[]{:S(2)}) copy-start(bf16[1,4,32,8,256]{4,3,2,1,0:T(8,128)(2,1)} %param.9) | copy-start | bytes 1572868
  139.7 7.8 %all-to-all-start = ((bf16[2,2,2,64,128]{4,3,1,0,2:T(8,128)(2,1)}), bf16[2,2,2,64,128]{4,3,1,0,2:T(8,128)(2,1)S(1)}, u32[]{:S(2)}, u32[]{:S(2)}) async-start(bf16[2,2,2,64,128]{4,3,1,0,2:T(8,128)(2,1)} %copy.24), calls=%async_computation | async-start | bytes 262144 | tf_op jit(solution)/shard_map/all_to_all | solution.py:178
  143.1 54.4 %all-gather.3.cloned.1.call-start = ((), (), s32[]{:S(2)}) async-start(), calls=%async_computation.2 | async-start | bytes 2228224 | tf_op jit(solution)/shard_map/all_gather | solution.py:197
  200.5 1.6 copy-start.1
  200.6 2.2 copy-start.3
  200.6 2.8 %copy-start.5 = (bf16[32,64,1,512]{3,1,2,0:T(8,128)(2,1)S(1)}, bf16[32,64,1,512]{3,1,2,0:T(8,128)(2,1)}, u32[]{:S(2)}) copy-start(bf16[32,64,1,512]{3,1,2,0:T(8,128)(2,1)} %copy-done.4) | copy-start | bytes 6291460
Sparse Core Ops, SparseCore 0:
  37.6 100.4 all-reduce.2
  157.6 39.7 all-gather.2

commit v2 on v1

--- a/solution.py
+++ b/solution.py
@@ -144,57 +144,229 @@
     return sum0, sum1
 
 
-def cycle_kernel(spacing, scal_ref, x_ref, left_ref, back_ref, right_ref, right_t_ref, vis_ref, y_ref, res_ref):
+def cycle_kernel(
+    spacing, scal_ref, x_ref, left_ref, back_ref, right_ref, right_t_ref, vis_ref,
+    g_ref, res_ref,
+    core_sum, row_recv, row_sum, z_recv, full, turned, send, recv,
+):
+    chunks, cores, rows, depth = x_ref.shape[:4]
+    pairs = full.shape[1]
+    ratio = SG // CS
+    facet, row, sub = lax.axis_index("facet"), lax.axis_index("row"), lax.axis_index("sub")
+    core, z = lax.rem(facet, cores), facet // cores
+    other = {"facet": facet + 1 - 2 * core}
+
+    def row_peer(d):
+        return {"row": lax.rem(row + d, rows)}
+
+    def z_place(d):
+        return lax.rem(z + d, depth)
+
+    def z_peer(d):
+        return {"facet": z_place(d) * cores + core}
+
+    def sub_place(d):
+        return lax.rem(sub + d, pairs)
+
+    def sub_peer(d):
+        return {"sub": sub_place(d)}
+
+    peers = [other]
+    peers += [row_peer(d) for d in range(1, rows)]
+    peers += [z_peer(d) for d in range(1, depth)]
+    peers += [sub_peer(d) for d in range(1, pairs)]
+    barrier = pltpu.get_barrier_semaphore()
+    for peer in peers:
+        pl.semaphore_signal(barrier, inc=1, device_id=peer, device_id_type=pl.DeviceIdType.MESH)
+    pl.semaphore_wait(barrier, len(peers))
+
+    row_at, z_at, sub_at = 1, rows, rows + depth - 1
+    started = []
+
+    def send_to(way, chunk, slot, source, target, peer):
+        copy = pltpu.make_async_remote_copy(
+            src_ref=source,
+            dst_ref=target,
+            send_sem=send.at[way, chunk, slot],
+            recv_sem=recv.at[way, chunk, slot],
+            device_id=peer,
+            device_id_type=pl.DeviceIdType.MESH,
+        )
+        copy.start()
+        started.append(copy)
+        return copy
+
+    def core_start(c):
+        return [send_to(0, c, 0, x_ref.at[c, 1 - core], core_sum.at[c], other)]
+
+    def row_start(c):
+        @pl.loop(0, rows * depth)
+        def _(i):
+            r, p = i // depth, lax.rem(i, depth)
+            total = core_sum[c, r, p].astype(F32) + x_ref[c, core, r, p].astype(F32)
+            core_sum[c, r, p] = total.astype(BF16)
+
+        return [
+            send_to(
+                0, c, row_at + d - 1,
+                core_sum.at[c, lax.rem(row + d, rows)], row_recv.at[c, d - 1], row_peer(d),
+            )
+            for d in range(1, rows)
+        ]
+
+    def z_start(c):
+        @pl.loop(0, depth)
+        def _(p):
+            total = core_sum[c, row, p].astype(F32)
+            for d in range(1, rows):
+                total += row_recv[c, d - 1, p].astype(F32)
+            row_sum[c, p] = total.astype(BF16)
+
+        return [
+            send_to(
+                0, c, z_at + d - 1, row_sum.at[c, z_place(d)], z_recv.at[c, d - 1], z_peer(d)
+            )
+            for d in range(1, depth)
+        ]
+
+    def sub_start(c):
+        total = row_sum[c, z].astype(F32)
+        for d in range(1, depth):
+            total += z_recv[c, d - 1].astype(F32)
+        z_recv[c, 0] = total.astype(BF16)
+        full[c, sub] = z_recv[c, 0, pl.ds(pl.multiple_of(sub * CS, CS), CS)]
+        return [
+            send_to(
+                0, c, sub_at + d - 1,
+                z_recv.at[c, 0, pl.ds(pl.multiple_of(sub_place(d) * CS, CS), CS)],
+                full.at[c, sub], sub_peer(d),
+            )
+            for d in range(1, pairs)
+        ]
+
+    def wait(copies):
+        for copy in copies:
+            copy.wait_recv()
+
+    def run(stages):
+        flying = [[None] * chunks for _ in stages]
+        for c in range(chunks):
+            flying[0][c] = stages[0](c)
+        for step in range(chunks + len(stages) - 2):
+            for level in range(len(stages) - 1, 0, -1):
+                c = step - (level - 1)
+                if 0 <= c < chunks:
+                    wait(flying[level - 1][c])
+                    flying[level][c] = stages[level](c)
+        for c in range(chunks):
+            wait(flying[-1][c])
+
+    run([core_start, row_start, z_start, sub_start])
+
     tiles = vis_ref.shape[0]
-    rows = [scal_ref[2 + j] for j in range(tiles)]
+
+    def contrib(t, b):
+        return jnp.concatenate(
+            [full[t * ratio + a, b].astype(F32) for a in range(ratio)], axis=0
+        )
+
     out = subgrid_cycle(
-        scal_ref[0], spacing, rows, scal_ref[1],
-        lambda t, b: x_ref[t, b].astype(F32),
+        scal_ref[0], spacing, [scal_ref[2 + j] for j in range(tiles)], scal_ref[1], contrib,
         left_ref[...], back_ref[...], right_ref[...], right_t_ref[...],
         functools.partial(observe_tile, vis_ref, res_ref), None,
     )
     for t in range(TERMS):
-        for b in range(SG // CS):
-            y_ref[t, b] = out[t][b]
+        for b in range(ratio):
+            for a in range(ratio):
+                turned[t * ratio + a, b] = out[t][b][a * CS : (a + 1) * CS]
+
+    def mine(c):
+        return g_ref.at[c, core, row, z, pl.ds(pl.multiple_of(sub * CS, CS), CS)]
+
+    def back_sub(c):
+        g_ref[c, core, row, z, pl.ds(pl.multiple_of(sub * CS, CS), CS)] = turned[c, sub]
+        return [
+            send_to(1, c, sub_at + d - 1, turned.at[c, sub_place(d)], mine(c), sub_peer(d))
+            for d in range(1, pairs)
+        ]
+
+    def back_z(c):
+        return [
+            send_to(
+                1, c, z_at + d - 1,
+                g_ref.at[c, core, row, z], g_ref.at[c, core, row, z], z_peer(d),
+            )
+            for d in range(1, depth)
+        ]
+
+    def back_row(c):
+        return [
+            send_to(
+                1, c, row_at + d - 1, g_ref.at[c, core, row], g_ref.at[c, core, row], row_peer(d)
+            )
+            for d in range(1, rows)
+        ]
+
+    def back_core(c):
+        return [send_to(1, c, 0, g_ref.at[c, core], g_ref.at[c, core], other)]
+
+    run([back_sub, back_z, back_row, back_core])
+    for copy in started:
+        copy.wait_send()
+
+
+def exchange(partial, scal, tables, observed, spacing):
+    chunks, cores, rows, depth, span, lanes = partial.shape
+    pairs = span // CS
+    vmem = pl.BlockSpec(memory_space=pltpu.VMEM)
+    slots = rows + depth + pairs - 2
+    return pl.pallas_call(
+        functools.partial(cycle_kernel, spacing),
+        out_shape=(
+            jax.ShapeDtypeStruct(partial.shape, BF16),
+            jax.ShapeDtypeStruct(observed.shape, BF16),
+        ),
+        in_specs=[pl.BlockSpec(memory_space=pltpu.SMEM)] + [vmem] * 6,
+        out_specs=(vmem, vmem),
+        scratch_shapes=[
+            pltpu.VMEM((chunks, rows, depth, span, lanes), BF16),
+            pltpu.VMEM((chunks, rows - 1, depth, span, lanes), BF16),
+            pltpu.VMEM((chunks, depth, span, lanes), BF16),
+            pltpu.VMEM((chunks, depth - 1, span, lanes), BF16),
+            pltpu.VMEM((chunks, pairs, CS, lanes), BF16),
+            pltpu.VMEM((chunks, pairs, CS, lanes), BF16),
+            pltpu.SemaphoreType.DMA((2, chunks, slots)),
+            pltpu.SemaphoreType.DMA((2, chunks, slots)),
+        ],
+        compiler_params=pltpu.CompilerParams(
+            collective_id=0, has_side_effects=True, vmem_limit_bytes=56 * 2**20
+        ),
+    )(scal, partial, *tables, observed)
 
 
 def local(facet_model, sub_offsets, tile_rows, tile_counts, visibilities):
     terms, facets, rows_here, pixels = facet_model.shape
     spacing = SKY // pixels
-    ratio = SG // CS
-    pairs = lax.axis_size("sub")
-    pair = lax.axis_index("sub")
+    rows, pairs = lax.axis_size("row"), lax.axis_size("sub")
+    cores = 2
+    depth = lax.axis_size("facet") // cores
     strip_group = lax.axis_index(("facet", "row"))
-    owner = strip_group * pairs + pair
+    owner = strip_group * pairs + lax.axis_index("sub")
     columns = column_table(pixels)
-    real, imag = row_table(sub_offsets, pixels, strip_group * rows_here, rows_here)
+    offsets = sub_offsets.reshape(depth, cores, rows, pairs).transpose(1, 2, 0, 3).reshape(-1)
+    real, imag = row_table(offsets, pixels, strip_group * rows_here, rows_here)
     table = jnp.stack([real, imag], axis=2)
     strips = jnp.einsum(
         "tfpq,nq->tfpn", facet_model, columns, preferred_element_type=F32
     ).astype(BF16)
     both = jnp.stack([strips, times_i(strips)], axis=2)
     partial = jnp.einsum("skzp,tfzpn->tfskn", table, both, preferred_element_type=F32).astype(BF16)
-    summed = lax.psum_scatter(partial, ("facet", "row"), scatter_dimension=2, tiled=True)
-    contrib = lax.all_to_all(summed, "sub", split_axis=2, concat_axis=1, tiled=True)
-    contrib = contrib.reshape(terms, ratio, SG, 2 * CS)
-    left, back, right, right_t = grid_tables()
+    partial = partial.reshape(terms * facets, cores, rows, depth, pairs * CS, 2 * CS)
     scal = jnp.concatenate(
         [lax.dynamic_slice(sub_offsets, (owner,), (1,)) % spacing, tile_counts, tile_rows[0]]
     )
-    vmem = pl.BlockSpec(memory_space=pltpu.VMEM)
-    returned, residual = pl.pallas_call(
-        functools.partial(cycle_kernel, spacing),
-        out_shape=(
-            jax.ShapeDtypeStruct(contrib.shape, BF16),
-            jax.ShapeDtypeStruct(visibilities.shape[1:], BF16),
-        ),
-        in_specs=[pl.BlockSpec(memory_space=pltpu.SMEM)] + [vmem] * 6,
-        out_specs=(vmem, vmem),
-        compiler_params=pltpu.CompilerParams(vmem_limit_bytes=32 * 2**20),
-    )(scal, contrib, left, back, right, right_t, visibilities[0])
-    returned = returned.reshape(terms, facets * pairs, 1, CS, 2 * CS)
-    received = lax.all_to_all(returned, "sub", split_axis=1, concat_axis=2, tiled=True)
-    turned = lax.all_gather(received, ("facet", "row"), axis=2, tiled=True)
+    turned, residual = exchange(partial, scal, grid_tables(), visibilities[0], spacing)
+    turned = turned.reshape(terms, facets, sub_offsets.shape[0], CS, 2 * CS)
     pairs_of = jnp.stack([turned, -times_i(turned)], axis=4)
     strip_round = jnp.einsum(
         "skzp,tfskzn->tfpn", table, pairs_of, preferred_element_type=F32

time: 227 us -> 127 us (0.56)
  waiting for transfers between devices: 138 us -> 0 us
  Pallas kernels: 2.38 us -> 63.9 us
  between operations: 17.6 us -> 3.43 us
  blocking collectives: 6.85 us -> 0 us
  starting transfers between devices: 3.46 us -> 0 us
  other arithmetic: 14 us -> 16.5 us
    unnamed x3 -> x0, waiting for transfers between devices: 94.1 us -> none
    pallas_call x1, Pallas kernels: 2.38 us -> 63.9 us  [exchange(): pl.pallas_call(functools.partial(cycle_kernel, spacing), out_shape=(jax.S...]
    all_gather x1 -> x0, waiting for transfers between devices: 39.9 us -> none  [local(): turned = lax.all_gather(received, ('facet', 'row'), axis=2, tiled=True)]
    all_to_all x1 -> x0, blocking collectives: 6.85 us -> none  [local(): lax.all_to_all(returned, 'sub', split_axis=1, concat_axis=2, tiled=True)]
    all_to_all x1 -> x0, waiting for transfers between devices: 4.32 us -> none  [local(): lax.all_to_all(summed, 'sub', split_axis=2, concat_axis=1, tiled=True)]
    all_to_all x1 -> x0, starting transfers between devices: 3.38 us -> none  [local(): lax.all_to_all(summed, 'sub', split_axis=2, concat_axis=1, tiled=True)]
    unnamed x20 -> x11, local copies, waits for them, and re-layouts: 5.62 us -> 3.2 us
  transfers between devices with their start and end apart: 3 -> 0, of which waited for: 3 -> 0; matrix products, arithmetic and copies ran while one was open for 1% -> 0% of each run, Pallas kernels for 0% -> 0%
where the time goes in v2:
time: 127 us; the launch traced here: 126 us
  Pallas kernels  63.9 us (50%)
  matrix products  36.5 us (29%)
  other arithmetic  16.5 us (13%)
  local copies, waits for them, and re-layouts  6.14 us (5%)
  between operations  3.43 us (3%)
    pallas_call x1, Pallas kernels, exchange(): pl.pallas_call(functools.partial(cycle_kernel, spacing), out_shape=(jax.S...  63.9 us
    dot_general x1, matrix products, local(): jnp.einsum('tfpq,nq->tfpn', facet_model, columns, preferred_element_type=...  16.2 us
    dot_general x1, matrix products, local(): jnp.einsum('tfpn,nq->tfpq', strip_round, columns, preferred_element_type=...  14.2 us
    dot_general x1, matrix products, local(): jnp.einsum('skzp,tfzpn->tfskn', table, both, preferred_element_type=F32)  3.64 us
    another operation x1, other arithmetic  3.41 us
    unnamed x11, local copies, waits for them, and re-layouts  3.2 us
    concatenate x1, other arithmetic, times_i(): return jnp.concatenate([-value[..., half:], value[..., :half]], axis=-1)  3.09 us
    convert_element_type x1, other arithmetic, row_table(): return (real.astype(BF16), imag.astype(BF16))  2.65 us

profile of v2, /device:TPU:0, one launch (start us, length us, event | category | flops | bytes accessed | tf_op | source)
XLA Modules:
  0.0 126.4 jit_solution(17933874966020036944)
XLA Ops:
  1.3 1.2 dynamic_slice.3
  4.5 1.3 %pad_add_fusion.scal_ref = s32[6]{0:T(128)} fusion(s32[4]{0:T(128)} %bitcast.83, s32[1]{0:T(128)S(6)} %copy.39, s32[1]{0:T(128)S(6)} %select_n.63), kind=kLoop, calls=%fused_computation.119 | loop fusion | flops 12 | bytes 48 | tf_op jit(solution)/shard_map/concatenate | solution.py:365
  5.8 0.1 add.225
  5.9 0.7 reshape.163
  6.7 0.1 mul.468
  6.8 0.3 fusion.57
  7.1 0.1 fusion.46
  7.2 0.3 multiply_convert_fusion
  7.7 0.0 copy-start.3
  7.7 0.2 fusion.53
  7.9 0.2 fusion.55
  8.1 0.6 multiply_convert_fusion.3
  8.7 0.7 pad_maximum_fusion.4
  9.4 0.3 fusion.48
  9.7 0.8 copy.14
  10.5 0.6 sine_multiply_fusion
  11.1 2.7 %subtract_convert_fusion = (bf16[32,64,1,512]{3,1,2,0:T(8,128)(2,1)S(1)}, bf16[32,64,1,512]{3,1,2,0:T(8,128)(2,1)}) fusion(f32[64,512]{1,0:T(8,128)S(1)} %get-tuple-element.21, f32[32,512]{1,0:T(8,128)S(1)} %get-tuple-element.20, f32[64,512]{1,0:T(8,128)S(1)} %get-tuple-element.19, f32[32,512]{1,0:T(8,128)S(1)} %get-tuple-element.18), kind=kLoop, calls=%fused_computation.10 | loop fusion | flops 8388608 | bytes 4587520 | tf_op jit(solution)/shard_map/convert_element_type | solution.py:59
  13.7 0.0 copy-done.3
  13.7 1.1 multiply_subtract_fusion
  14.9 3.4 %fusion.7 = (bf16[64,8192]{1,0:T(8,128)(2,1)S(1)}, bf16[64,8192]{1,0:T(8,128)(2,1)S(1)}) fusion(f32[8,8,64,128]{3,2,1,0:T(8,128)S(1)} %bitcast.71, f32[8192]{0:T(1024)S(1)} %bitcast.81, f32[8,8,64,128]{3,2,1,0:T(8,128)S(1)} %bitcast.72), kind=kLoop, calls=%fused_computation.15 | loop fusion | flops 2097152 | bytes 6324224 | tf_op jit(solution)/shard_map/convert
  18.3 16.2 %fusion.12 = bf16[128,2,2,512]{3,0,2,1:T(8,128)(2,1)S(1)} fusion(bf16[2,2,512,8192]{3,2,1,0:T(8,128)(2,1)} %param.5, bf16[64,8192]{1,0:T(8,128)(2,1)S(1)} %get-tuple-element.35, bf16[64,8192]{1,0:T(8,128)(2,1)S(1)} %get-tuple-element.34), kind=kOutput, calls=%fused_computation.24 | convolution fusion | flops 4299423744 | bytes 36175872 | tf_op jit(solution)/shard_map/tfpq,nq->tfpn/dot_general | solution.py:359
  34.5 0.0 copy-start.1
  34.6 1.5 %copy-done.1 = bf16[32,64,1,512]{3,1,2,0:T(8,128)(2,1)S(1)} copy-done((bf16[32,64,1,512]{3,1,2,0:T(8,128)(2,1)S(1)}, bf16[32,64,1,512]{3,1,2,0:T(8,128)(2,1)}, u32[]{:S(2)}) %copy-start.1) | copy-done | bytes 2097176
  36.1 3.6 %bitcast_convert_fusion = bf16[2,2,128,32,64]{2,4,3,1,0:T(8,128)(2,1)} fusion(bf16[32,64,1,512]{3,1,2,0:T(8,128)(2,1)S(1)} %copy-done.1, bf16[32,64,1,512]{3,1,2,0:T(8,128)(2,1)S(1)} %get-tuple-element.28, bf16[2,2,1,512,128]{3,4,1,0,2:T(8,128)(2,1)S(1)} %maximum_bitcast_fusion.6, bf16[2,2,1,512,128]{3,4,1,0,2:T(8,128)(2,1)S(1)} %bitcast.70), kind=kOutput, calls=%fused_computation.5 | convolution fusion | flops 2157445120 | bytes 7340032 | tf_op jit(solution)/shard_map/skzp,tfzpn->tfskn/dot_general | solution.py:363
  39.8 63.9 %shard_map.68 = (bf16[4,2,2,4,128,128]{5,4,3,2,1,0:T(8,128)(2,1)}, bf16[4,32,8,256]{3,2,1,0:T(8,128)(2,1)}) custom-call(s32[6]{0:T(128)} %pad_add_fusion.scal_ref, bf16[4,2,2,4,128,128]{5,4,3,2,1,0:T(8,128)(2,1)} %bitcast.75, bf16[128,256]{1,0:T(8,128)(2,1)} %get-tuple-element.52.left_ref, bf16[128,256]{1,0:T(8,128)(2,1)} %get-tuple-element.53.back_ref, ...), custom_call_target="tpu_custom_call" | custom-call | tf_op jit(solution)/shard_map/pallas_call | solution.py:323
  103.6 3.1 %fusion.8 = (bf16[2,2,32,64,1,64]{5,3,2,1,0,4:T(8,128)(2,1)S(1)}, bf16[2,2,32,64,1,64]{5,3,2,1,0,4:T(8,128)(2,1)S(1)}) fusion(bf16[2,2,32,64,128]{4,3,2,1,0:T(8,128)(2,1)} %bitcast.73), kind=kLoop, calls=%fused_computation.18 | loop fusion | flops 524288 | bytes 4194304 | tf_op jit(solution)/shard_map/concatenate | solution.py:80
  106.7 0.0 copy-start
  106.7 0.0 copy-start.2
  106.7 1.3 %maximum_negate_fusion = bf16[2,2,32,64,1,128]{5,3,2,1,0,4:T(8,128)(2,1)S(1)} fusion(bf16[2,2,32,64,1,64]{5,3,2,1,0,4:T(8,128)(2,1)S(1)} %get-tuple-element.25, bf16[2,2,32,64,1,64]{5,3,2,1,0,4:T(8,128)(2,1)S(1)} %get-tuple-element.24), kind=kLoop, calls=%fused_computation.20 | loop fusion | flops 5242880 | bytes 4194304 | tf_op jit(solution)/shard_map/neg | solution.py:370
  108.1 0.3 copy-done
  108.3 0.6 copy-done.2
  109.0 2.4 %fusion.2 = bf16[2,2,128,512,1,1]{2,3,4,0,1,5:T(8,128)(2,1)S(1)} fusion(bf16[32,64,1,512]{3,1,2,0:T(8,128)(2,1)S(1)} %copy-done.2, bf16[32,64,1,512]{3,1,2,0:T(8,128)(2,1)S(1)} %get-tuple-element.28, bf16[2,2,32,64,1,128]{5,3,2,1,0,4:T(8,128)(2,1)S(1)} %maximum_negate_fusion, bf16[2,2,32,64,1,128]{5,3,2,1,0,4:T(8,128)(2,1)S(1)} %bitcast.74), kind=kOutput, calls=%fused_computation.6 | convolution fusion | flops 2151677952 | bytes 8912896 | tf_op jit(solution)/shard_map/skzp,tfskzn->tfpn/dot_general | solution.py:371
  111.4 0.0 copy-start.4
  111.4 14.2 %convolution_convert_fusion = bf16[2,2,512,8192]{3,2,1,0:T(8,128)(2,1)} fusion(bf16[64,8192]{1,0:T(8,128)(2,1)S(1)} %get-tuple-element.35, bf16[64,8192]{1,0:T(8,128)(2,1)S(1)} %get-tuple-element.34, bf16[2,2,128,512,1,1]{2,3,4,0,1,5:T(8,128)(2,1)S(1)} %fusion.2), kind=kOutput, calls=%fused_computation | convolution fusion | flops 4315938816 | bytes 36175872 | tf_op jit(solution)/shard_map/tfpn,nq->tfpq/dot_general | solution.py:374
  125.6 0.0 copy-done.4
  125.6 0.8 copy.40
  (11 shorter events, 0.2 us)
Async XLA Ops:
  7.7 6.1 %copy-start.3 = (bf16[2,2,64,256]{3,2,1,0:T(8,128)(2,1)}, bf16[2,2,64,256]{3,2,1,0:T(8,128)(2,1)S(1)}, u32[]{:S(2)}) copy-start(bf16[2,2,64,256]{3,2,1,0:T(8,128)(2,1)S(1)} %copy.13) | copy-start | bytes 393220
  34.5 1.6 %copy-start.1 = (bf16[32,64,1,512]{3,1,2,0:T(8,128)(2,1)S(1)}, bf16[32,64,1,512]{3,1,2,0:T(8,128)(2,1)}, u32[]{:S(2)}) copy-start(bf16[32,64,1,512]{3,1,2,0:T(8,128)(2,1)} %get-tuple-element.29) | copy-start | bytes 6291460
  106.7 1.6 %copy-start = (bf16[4,2,2,4,128,128]{5,4,3,2,1,0:T(8,128)(2,1)S(1)}, bf16[4,2,2,4,128,128]{5,4,3,2,1,0:T(8,128)(2,1)}, u32[]{:S(2)}) copy-start(bf16[4,2,2,4,128,128]{5,4,3,2,1,0:T(8,128)(2,1)} %get-tuple-element.22) | copy-start | bytes 6291460
  106.7 2.2 %copy-start.2 = (bf16[32,64,1,512]{3,1,2,0:T(8,128)(2,1)S(1)}, bf16[32,64,1,512]{3,1,2,0:T(8,128)(2,1)}, u32[]{:S(2)}) copy-start(bf16[32,64,1,512]{3,1,2,0:T(8,128)(2,1)} %get-tuple-element.29) | copy-start | bytes 6291460
  111.4 14.3 %copy-start.4 = (bf16[4,32,8,256]{3,2,1,0:T(8,128)(2,1)S(1)}, bf16[4,32,8,256]{3,2,1,0:T(8,128)(2,1)}, u32[]{:S(2)}) copy-start(bf16[4,32,8,256]{3,2,1,0:T(8,128)(2,1)} %get-tuple-element.23) | copy-start | bytes 1572868

commit v3 on v2

--- a/solution.py
+++ b/solution.py
@@ -12,6 +12,7 @@
 CS = 64
 SG = 128
 TERMS = 2
+VMEM_LIMIT = 62 * 2**20
 
 two_pi = 2.0 * math.pi
 F32 = jnp.float32
@@ -23,40 +24,61 @@
     return jnp.cos(angle), jnp.sin(angle)
 
 
-def taper_of(places, pixels):
-    curve = jnp.sin(math.pi * (places.astype(F32) + 0.5) / pixels)
-    return (0.25 + 0.75 * curve * curve) / math.sqrt(pixels)
-
-
 def iota(count):
     return jnp.arange(count, dtype=jnp.int32)
 
 
-def column_table(pixels):
+def along(shape, axis):
+    return lax.broadcasted_iota(jnp.int32, shape, axis)
+
+
+def fill_columns(cols_ref, high_r, high_i, high_c, high_s):
+    pixels, lanes = cols_ref.shape
     spacing = SKY // pixels
-    freqs = spacing * iota(CS)
-    lane = 128
-    low = unit(freqs[:, None] * iota(lane)[None, :] % SKY, SKY)
-    high = unit(freqs[:, None] * (lane * iota(pixels // lane))[None, :] % SKY, SKY)
-    scale = taper_of(iota(pixels), pixels).reshape(pixels // lane, lane)
-    lr, li, hr, hi, scale = lax.optimization_barrier((*low, *high, scale))
-    lr, li, hr, hi = lr[:, None, :], li[:, None, :], hr[:, :, None], hi[:, :, None]
-    real = (hr * lr - hi * li) * scale
-    imag = (hr * li + hi * lr) * scale
-    return jnp.concatenate([real, imag], axis=0).astype(BF16).reshape(2 * CS, pixels)
-
-
-def row_table(offsets, pixels, first_row, count):
+    block = 128
+    count = pixels // block
+    freq = spacing * lax.rem(along((count, lanes), 1), CS)
+    high_r[...], high_i[...] = unit(freq * (block * along((count, lanes), 0)) % SKY, SKY)
+    step = block * along((count, lanes), 0).astype(F32) * (two_pi / pixels)
+    high_c[...], high_s[...] = jnp.cos(step), jnp.sin(step)
+    shape = (block, lanes)
+    low_r, low_i = unit(spacing * lax.rem(along(shape, 1), CS) * along(shape, 0) % SKY, SKY)
+    first = along(shape, 1) < CS
+    low = jnp.where(first, low_r, low_i)
+    low_j = jnp.where(first, -low_i, low_r)
+    part = (along(shape, 0).astype(F32) + 0.5) * (two_pi / pixels)
+    scale = 1.0 / math.sqrt(pixels)
+    part_c, part_s = jnp.cos(part) * (0.375 * scale), jnp.sin(part) * (0.375 * scale)
+
+    @pl.loop(0, count)
+    def _(h):
+        row = pl.ds(h, 1)
+        taper = 0.625 * scale - (high_c[row] * part_c - high_s[row] * part_s)
+        value = (high_r[row] * low + high_i[row] * low_j) * taper
+        cols_ref[pl.ds(pl.multiple_of(h * block, block), block)] = value.astype(BF16)
+
+
+def fill_rows(tab_ref, offsets, base_r, base_i, first_row, pixels):
+    count = base_r.shape[1]
+    subgrids = base_r.shape[0]
     spacing = SKY // pixels
-    places = first_row + iota(count)
-    base = unit(offsets[:, None] * places[None, :] % SKY, SKY)
-    step = unit(spacing * iota(CS)[:, None] * places[None, :] % SKY, SKY)
-    scale = taper_of(places, pixels)
-    br, bi, sr, si = lax.optimization_barrier((*base, step[0] * scale, step[1] * scale))
-    br, bi, sr, si = br[:, None, :], bi[:, None, :], sr[None], si[None]
-    real = br * sr - bi * si
-    imag = br * si + bi * sr
-    return real.astype(BF16), imag.astype(BF16)
+    shape = (CS, count)
+    place = first_row + along(shape, 1)
+    step_r, step_i = unit(spacing * along(shape, 0) * place % SKY, SKY)
+    curve = jnp.sin(math.pi * (place.astype(F32) + 0.5) / pixels)
+    scale = (0.25 + 0.75 * curve * curve) / math.sqrt(pixels)
+    step_r, step_i = step_r * scale, step_i * scale
+    base_r[...], base_i[...] = unit(
+        offsets * (first_row + along((subgrids, count), 1)) % SKY, SKY
+    )
+
+    @pl.loop(0, subgrids)
+    def _(s):
+        br, bi = base_r[pl.ds(s, 1)], base_i[pl.ds(s, 1)]
+        value = jnp.concatenate(
+            [br * step_r - bi * step_i, br * step_i + bi * step_r], axis=1
+        )
+        tab_ref[pl.ds(pl.multiple_of(s * CS, CS), CS)] = value.astype(BF16)
 
 
 def grid_tables():
@@ -145,11 +167,15 @@
 
 
 def cycle_kernel(
-    spacing, scal_ref, x_ref, left_ref, back_ref, right_ref, right_t_ref, vis_ref,
-    g_ref, res_ref,
-    core_sum, row_recv, row_sum, z_recv, full, turned, send, recv,
+    pixels, offset_ref, count_ref, place_ref, list_ref, fm_ref,
+    left_ref, back_ref, right_ref, right_t_ref, vis_ref,
+    strip_ref, res_ref, cols_ref,
+    x_ref, g_ref, core_sum, row_recv, row_sum, z_recv, full, turned, back_full,
+    buffer, both, tab, high_r, high_i, high_c, high_s, base_r, base_i, total_ref,
+    fetch, send, recv,
 ):
-    chunks, cores, rows, depth = x_ref.shape[:4]
+    spacing = SKY // pixels
+    chunks, depth, cores, rows, span, lanes = x_ref.shape
     pairs = full.shape[1]
     ratio = SG // CS
     facet, row, sub = lax.axis_index("facet"), lax.axis_index("row"), lax.axis_index("sub")
@@ -175,9 +201,25 @@
     peers += [row_peer(d) for d in range(1, rows)]
     peers += [z_peer(d) for d in range(1, depth)]
     peers += [sub_peer(d) for d in range(1, pairs)]
+    slots, tile = buffer.shape[:2]
+    rows_here = both.shape[0] // 2
+    tiles_each = rows_here // tile
+    steps = chunks * tiles_each
+
+    def load(step):
+        slot = lax.rem(step, slots)
+        return pltpu.make_async_copy(
+            fm_ref.at[pl.ds(pl.multiple_of(step * tile, tile), tile)],
+            buffer.at[slot],
+            fetch.at[slot],
+        )
+
+    for step in range(min(slots, steps)):
+        load(step).start()
     barrier = pltpu.get_barrier_semaphore()
     for peer in peers:
         pl.semaphore_signal(barrier, inc=1, device_id=peer, device_id_type=pl.DeviceIdType.MESH)
+    fill_columns(cols_ref, high_r, high_i, high_c, high_s)
     pl.semaphore_wait(barrier, len(peers))
 
     row_at, z_at, sub_at = 1, rows, rows + depth - 1
@@ -197,19 +239,48 @@
         return copy
 
     def core_start(c):
-        return [send_to(0, c, 0, x_ref.at[c, 1 - core], core_sum.at[c], other)]
+        @pl.loop(0, tiles_each)
+        def _(i):
+            step = c * tiles_each + i
+            load(step).wait()
+            strip = jnp.dot(
+                buffer[lax.rem(step, slots)], cols_ref[...], preferred_element_type=F32
+            )
+            at = pl.multiple_of(i * tile, tile)
+            both[pl.ds(at, tile)] = strip.astype(BF16)
+            both[pl.ds(rows_here + at, tile)] = times_i(strip).astype(BF16)
+
+            @pl.when(step + slots < steps)
+            def _():
+                load(step + slots).start()
+
+        if c == 0:
+            fill_rows(
+                tab, list_ref[...], base_r, base_i,
+                (facet * rows + row) * rows_here, pixels,
+            )
+
+        @pl.loop(0, depth * cores)
+        def _(i):
+            at = i * rows * span
+            value = dot(tab[pl.ds(pl.multiple_of(at, rows * span), rows * span)], both[...])
+            x_ref[c, i // cores, lax.rem(i, cores)] = value.astype(BF16).reshape(
+                rows, span, lanes
+            )
+
+        return [send_to(0, c, 0, x_ref.at[c, :, 1 - core], core_sum.at[c], other)]
 
     def row_start(c):
         @pl.loop(0, rows * depth)
         def _(i):
-            r, p = i // depth, lax.rem(i, depth)
-            total = core_sum[c, r, p].astype(F32) + x_ref[c, core, r, p].astype(F32)
-            core_sum[c, r, p] = total.astype(BF16)
+            p, r = i // rows, lax.rem(i, rows)
+            total = core_sum[c, p, r].astype(F32) + x_ref[c, p, core, r].astype(F32)
+            core_sum[c, p, r] = total.astype(BF16)
 
         return [
             send_to(
                 0, c, row_at + d - 1,
-                core_sum.at[c, lax.rem(row + d, rows)], row_recv.at[c, d - 1], row_peer(d),
+                core_sum.at[c, :, lax.rem(row + d, rows)], row_recv.at[c, d - 1], row_peer(d),
             )
             for d in range(1, rows)
         ]
@@ -217,7 +288,7 @@
     def z_start(c):
         @pl.loop(0, depth)
         def _(p):
-            total = core_sum[c, row, p].astype(F32)
+            total = core_sum[c, p, row].astype(F32)
             for d in range(1, rows):
                 total += row_recv[c, d - 1, p].astype(F32)
             row_sum[c, p] = total.astype(BF16)
@@ -250,13 +321,12 @@
 
     def run(stages):
         flying = [[None] * chunks for _ in stages]
-        for c in range(chunks):
-            flying[0][c] = stages[0](c)
-        for step in range(chunks + len(stages) - 2):
-            for level in range(len(stages) - 1, 0, -1):
-                c = step - (level - 1)
+        for step in range(chunks + len(stages) - 1):
+            for level in range(len(stages) - 1, -1, -1):
+                c = step - level
                 if 0 <= c < chunks:
-                    wait(flying[level - 1][c])
+                    if level:
+                        wait(flying[level - 1][c])
                     flying[level][c] = stages[level](c)
         for c in range(chunks):
             wait(flying[-1][c])
@@ -270,8 +340,10 @@
             [full[t * ratio + a, b].astype(F32) for a in range(ratio)], axis=0
         )
 
+    owner = (facet * rows + row) * pairs + sub
     out = subgrid_cycle(
-        scal_ref[0], spacing, [scal_ref[2 + j] for j in range(tiles)], scal_ref[1], contrib,
+        lax.rem(offset_ref[owner], spacing), spacing, [place_ref[0, j] for j in range(tiles)],
+        count_ref[0], contrib,
         left_ref[...], back_ref[...], right_ref[...], right_t_ref[...],
         functools.partial(observe_tile, vis_ref, res_ref), None,
     )
@@ -280,101 +352,143 @@
             for a in range(ratio):
                 turned[t * ratio + a, b] = out[t][b][a * CS : (a + 1) * CS]
 
-    def mine(c):
-        return g_ref.at[c, core, row, z, pl.ds(pl.multiple_of(sub * CS, CS), CS)]
-
     def back_sub(c):
-        g_ref[c, core, row, z, pl.ds(pl.multiple_of(sub * CS, CS), CS)] = turned[c, sub]
+        back_full[c, sub] = turned[c, sub]
         return [
-            send_to(1, c, sub_at + d - 1, turned.at[c, sub_place(d)], mine(c), sub_peer(d))
+            send_to(1, c, sub_at + d - 1, turned.at[c, sub_place(d)], back_full.at[c, sub], sub_peer(d))
             for d in range(1, pairs)
         ]
 
     def back_z(c):
-        return [
-            send_to(
-                1, c, z_at + d - 1,
-                g_ref.at[c, core, row, z], g_ref.at[c, core, row, z], z_peer(d),
-            )
-            for d in range(1, depth)
-        ]
+        block = jnp.concatenate([back_full[c, q].astype(F32) for q in range(pairs)], axis=0)
+        g_ref[c, z, core, row] = block.T.astype(BF16)
+        mine = g_ref.at[c, z, core, row]
+        return [send_to(1, c, z_at + d - 1, mine, mine, z_peer(d)) for d in range(1, depth)]
 
     def back_row(c):
-        return [
-            send_to(
-                1, c, row_at + d - 1, g_ref.at[c, core, row], g_ref.at[c, core, row], row_peer(d)
-            )
-            for d in range(1, rows)
-        ]
+        mine = g_ref.at[c, :, core, row]
+        return [send_to(1, c, row_at + d - 1, mine, mine, row_peer(d)) for d in range(1, rows)]
 
     def back_core(c):
-        return [send_to(1, c, 0, g_ref.at[c, core], g_ref.at[c, core], other)]
+        mine = g_ref.at[c, :, core]
+        return [send_to(1, c, 0, mine, mine, other)]
 
     run([back_sub, back_z, back_row, back_core])
+
+    total_ref[...] = jnp.zeros_like(total_ref)
+
+    @pl.loop(0, depth * cores * rows)
+    def _(i):
+        p, h, r = i // (cores * rows), lax.rem(i // rows, cores), lax.rem(i, rows)
+        block = jnp.concatenate([g_ref[c, p, h, r] for c in range(chunks)], axis=0)
+        halves = [block[q * CS : (q + 1) * CS] for q in range(2 * chunks)]
+        swapped = []
+        for c in range(chunks):
+            swapped += [halves[2 * c + 1], -halves[2 * c]]
+        rows_at = tab[pl.ds(pl.multiple_of(i * span, span), span)]
+        total_ref[...] += dot(block, rows_at[:, :rows_here]) + dot(
+            jnp.concatenate(swapped, axis=0), rows_at[:, rows_here:]
+        )
+
+    for c in range(chunks):
+        strip_ref[c] = total_ref[c * lanes : (c + 1) * lanes].T.astype(BF16)
     for copy in started:
         copy.wait_send()
 
 
-def exchange(partial, scal, tables, observed, spacing):
-    chunks, cores, rows, depth, span, lanes = partial.shape
-    pairs = span // CS
+def exchange(facet_rows, sub_offsets, tile_counts, tile_rows, tables, observed, chunks, dims):
+    rows, depth, pairs = dims
+    cores = 2
+    pixels = facet_rows.shape[1]
+    rows_here = facet_rows.shape[0] // chunks
+    subgrids = sub_offsets.shape[0]
+    span, lanes = pairs * CS, 2 * CS
+    tile = math.gcd(rows_here, 256)
     vmem = pl.BlockSpec(memory_space=pltpu.VMEM)
+    smem = pl.BlockSpec(memory_space=pltpu.SMEM)
     slots = rows + depth + pairs - 2
+    whole = (chunks, depth, cores, rows, span, lanes)
     return pl.pallas_call(
-        functools.partial(cycle_kernel, spacing),
+        functools.partial(cycle_kernel, pixels),
         out_shape=(
-            jax.ShapeDtypeStruct(partial.shape, BF16),
+            jax.ShapeDtypeStruct((chunks, rows_here, lanes), BF16),
             jax.ShapeDtypeStruct(observed.shape, BF16),
+            jax.ShapeDtypeStruct((pixels, lanes), BF16),
         ),
-        in_specs=[pl.BlockSpec(memory_space=pltpu.SMEM)] + [vmem] * 6,
-        out_specs=(vmem, vmem),
+        in_specs=[smem] * 3 + [vmem, pl.BlockSpec(memory_space=pl.ANY)] + [vmem] * 5,
+        out_specs=(vmem, vmem, vmem),
         scratch_shapes=[
-            pltpu.VMEM((chunks, rows, depth, span, lanes), BF16),
+            pltpu.VMEM(whole, BF16),
+            pltpu.VMEM((*whole[:4], lanes, span), BF16),
+            pltpu.VMEM((chunks, depth, rows, span, lanes), BF16),
             pltpu.VMEM((chunks, rows - 1, depth, span, lanes), BF16),
             pltpu.VMEM((chunks, depth, span, lanes), BF16),
             pltpu.VMEM((chunks, depth - 1, span, lanes), BF16),
             pltpu.VMEM((chunks, pairs, CS, lanes), BF16),
             pltpu.VMEM((chunks, pairs, CS, lanes), BF16),
+            pltpu.VMEM((chunks, pairs, CS, lanes), BF16),
+            pltpu.VMEM((3, tile, pixels), BF16),
+            pltpu.VMEM((2 * rows_here, lanes), BF16),
+            pltpu.VMEM((subgrids * CS, 2 * rows_here), BF16),
+            pltpu.VMEM((pixels // 128, lanes), F32),
+            pltpu.VMEM((pixels // 128, lanes), F32),
+            pltpu.VMEM((pixels // 128, lanes), F32),
+            pltpu.VMEM((pixels // 128, lanes), F32),
+            pltpu.VMEM((subgrids, rows_here), F32),
+            pltpu.VMEM((subgrids, rows_here), F32),
+            pltpu.VMEM((chunks * lanes, rows_here), F32),
+            pltpu.SemaphoreType.DMA((3,)),
             pltpu.SemaphoreType.DMA((2, chunks, slots)),
             pltpu.SemaphoreType.DMA((2, chunks, slots)),
         ],
         compiler_params=pltpu.CompilerParams(
-            collective_id=0, has_side_effects=True, vmem_limit_bytes=56 * 2**20
+            collective_id=0, has_side_effects=True, vmem_limit_bytes=VMEM_LIMIT
         ),
-    )(scal, partial, *tables, observed)
+    )(
+        sub_offsets, tile_counts, tile_rows, sub_offsets.reshape(subgrids, 1),
+        facet_rows, *tables, observed,
+    )
+
+
+def spread_kernel(strip_ref, cols_ref, out_ref):
+    pixels = cols_ref.shape[0]
+    block = 1024
+
+    @pl.loop(0, pixels // block)
+    def _(i):
+        at = pl.ds(pl.multiple_of(i * block, block), block)
+        out_ref[:, at] = lax.dot_general(
+            strip_ref[...], cols_ref[at], (((1,), (1,)), ((), ())), preferred_element_type=F32
+        ).astype(BF16)
+
+
+def spread(strips, columns):
+    count, lanes = strips.shape
+    pixels = columns.shape[0]
+    tile = math.gcd(count, 256)
+    return pl.pallas_call(
+        spread_kernel,
+        grid=(count // tile,),
+        out_shape=jax.ShapeDtypeStruct((count, pixels), BF16),
+        in_specs=[
+            pl.BlockSpec((tile, lanes), lambda i: (i, 0)),
+            pl.BlockSpec((pixels, lanes), lambda i: (0, 0)),
+        ],
+        out_specs=pl.BlockSpec((tile, pixels), lambda i: (i, 0)),
+        compiler_params=pltpu.CompilerParams(vmem_limit_bytes=32 * 2**20),
+    )(strips, columns)
 
 
 def local(facet_model, sub_offsets, tile_rows, tile_counts, visibilities):
     terms, facets, rows_here, pixels = facet_model.shape
-    spacing = SKY // pixels
-    rows, pairs = lax.axis_size("row"), lax.axis_size("sub")
-    cores = 2
-    depth = lax.axis_size("facet") // cores
-    strip_group = lax.axis_index(("facet", "row"))
-    owner = strip_group * pairs + lax.axis_index("sub")
-    columns = column_table(pixels)
-    offsets = sub_offsets.reshape(depth, cores, rows, pairs).transpose(1, 2, 0, 3).reshape(-1)
-    real, imag = row_table(offsets, pixels, strip_group * rows_here, rows_here)
-    table = jnp.stack([real, imag], axis=2)
-    strips = jnp.einsum(
-        "tfpq,nq->tfpn", facet_model, columns, preferred_element_type=F32
-    ).astype(BF16)
-    both = jnp.stack([strips, times_i(strips)], axis=2)
-    partial = jnp.einsum("skzp,tfzpn->tfskn", table, both, preferred_element_type=F32).astype(BF16)
-    partial = partial.reshape(terms * facets, cores, rows, depth, pairs * CS, 2 * CS)
-    scal = jnp.concatenate(
-        [lax.dynamic_slice(sub_offsets, (owner,), (1,)) % spacing, tile_counts, tile_rows[0]]
+    chunks = terms * facets
+    dims = (lax.axis_size("row"), lax.axis_size("facet") // 2, lax.axis_size("sub"))
+    strips, residual, columns = exchange(
+        facet_model.reshape(chunks * rows_here, pixels), sub_offsets, tile_counts, tile_rows,
+        grid_tables(), visibilities[0], chunks, dims,
     )
-    turned, residual = exchange(partial, scal, grid_tables(), visibilities[0], spacing)
-    turned = turned.reshape(terms, facets, sub_offsets.shape[0], CS, 2 * CS)
-    pairs_of = jnp.stack([turned, -times_i(turned)], axis=4)
-    strip_round = jnp.einsum(
-        "skzp,tfskzn->tfpn", table, pairs_of, preferred_element_type=F32
-    ).astype(BF16)
-    residual_facets = jnp.einsum(
-        "tfpn,nq->tfpq", strip_round, columns, preferred_element_type=F32
-    ).astype(BF16)
-    return (residual_facets, residual[None])
+    residual_facets = spread(strips.reshape(chunks * rows_here, 2 * CS), columns)
+    return (residual_facets.reshape(facet_model.shape), residual[None])
 
 
 def solution(mesh):

time: 127 us -> 114 us (0.90)
  Pallas kernels: 63.9 us -> 104 us
  matrix products: 36.5 us -> 0 us
  other arithmetic: 16.5 us -> 1.95 us
  between operations: 3.43 us -> 1.36 us
    pallas_call x1 -> x2, Pallas kernels: 63.9 us -> 104 us  [the longest x1 82.5 us: exchange(): pl.pallas_call(functools.partial(cycle_kernel, pixels), out_shape=(jax.Sh...]
    dot_general x4 -> x0, matrix products: 36.5 us -> none  [the longest x1 16.2 us: local(): jnp.einsum('tfpq,nq->tfpn', facet_model, columns, preferred_element_type=...]
    concatenate x2 -> x0, other arithmetic: 4.37 us -> none  [the longest x1 3.09 us: times_i(): return jnp.concatenate([-value[..., half:], value[..., :half]], axis=-1)]
    another operation x2 -> x0, other arithmetic: 3.45 us -> none
    convert_element_type x1 -> x0, other arithmetic: 2.65 us -> none  [row_table(): return (real.astype(BF16), imag.astype(BF16))]
    neg x2 -> x0, other arithmetic: 1.34 us -> none  [the longest x1 1.3 us: local(): pairs_of = jnp.stack([turned, -times_i(turned)], axis=4)]
    unnamed x11 -> x9, local copies, waits for them, and re-layouts: 3.2 us -> 3.43 us
where the time goes in v3:
time: 114 us; the launch traced here: 113 us
  Pallas kernels  104 us (91%)
  local copies, waits for them, and re-layouts  5.61 us (5%)
  other arithmetic  1.95 us (2%)
  between operations  1.36 us (1%)
    pallas_call x1, Pallas kernels, exchange(): pl.pallas_call(functools.partial(cycle_kernel, pixels), out_shape=(jax.Sh...  82.5 us
    pallas_call x1, Pallas kernels, spread(): pl.pallas_call(spread_kernel, grid=(count // tile,), out_shape=jax.ShapeD...  21.3 us
    unnamed x9, local copies, waits for them, and re-layouts  3.43 us

profile of v3, /device:TPU:0, one launch (start us, length us, event | category | flops | bytes accessed | tf_op | source)
XLA Modules:
  0.0 112.8 jit_solution(10086936177176811562)
XLA Ops:
  1.3 0.1 add.96
  1.4 1.3 %copy.12.list_ref = s32[32,1]{1,0:T(8,128)} copy(s32[32,1]{0,1:T(1,128)} %bitcast.20) | data formatting | bytes 256 | tf_op jit(solution)/shard_map/reshape | solution.py:448
  2.7 0.3 fusion.18
  3.0 0.3 multiply_convert_fusion
  3.5 0.0 copy-start.2
  3.5 0.6 multiply_convert_fusion.3
  4.1 0.7 pad_maximum_fusion.1
  4.7 0.8 copy.11
  5.5 0.0 copy-done.2
  5.5 82.5 %shard_map.68 = (bf16[4,512,128]{2,1,0:T(8,128)(2,1)}, bf16[4,32,8,256]{3,2,1,0:T(8,128)(2,1)}, bf16[8192,128]{1,0:T(8,128)(2,1)}) custom-call(s32[32]{0:T(128)} %offset_ref.1, s32[1]{0:T(128)S(6)} %copy.14.count_ref, s32[1,4]{1,0:T(1,128)} %place_ref.1, s32[32,1]{1,0:T(8,128)} %copy.12.list_ref, bf16[2048,8192]{1,0:T(8,128)(2,1)} %bitcast.13, ...), custom_call_target="tpu_custom_call" | custom-call | tf_op jit(solution)/shard_map/pallas_call | solution.py:411
  88.0 0.0 copy-start
  88.0 1.6 %copy-done = bf16[8192,128]{1,0:T(8,128)(2,1)S(1)} copy-done((bf16[8192,128]{1,0:T(8,128)(2,1)S(1)}, bf16[8192,128]{1,0:T(8,128)(2,1)}, u32[]{:S(2)}) %copy-start) | copy-done | bytes 2097176
  89.6 0.0 copy-start.1
  89.6 1.0 copy-done.1
  90.7 0.0 copy-start.3
  90.7 21.3 %shard_map.69 = bf16[2048,8192]{1,0:T(8,128)(2,1)} custom-call(bf16[2048,128]{1,0:T(8,128)(2,1)S(1)} %bitcast.12, bf16[8192,128]{1,0:T(8,128)(2,1)S(1)} %copy-done), custom_call_target="tpu_custom_call" | custom-call | tf_op jit(solution)/shard_map/pallas_call | solution.py:469
  112.0 0.0 copy-done.3
  112.0 0.8 copy.15
  (5 shorter events, 0.1 us)
Async XLA Ops:
  3.5 2.0 %copy-start.2 = (bf16[2,2,64,256]{3,2,1,0:T(8,128)(2,1)}, bf16[2,2,64,256]{3,2,1,0:T(8,128)(2,1)S(1)}, u32[]{:S(2)}) copy-start(bf16[2,2,64,256]{3,2,1,0:T(8,128)(2,1)S(1)} %copy.10) | copy-start | bytes 393220
  88.0 1.6 %copy-start = (bf16[8192,128]{1,0:T(8,128)(2,1)S(1)}, bf16[8192,128]{1,0:T(8,128)(2,1)}, u32[]{:S(2)}) copy-start(bf16[8192,128]{1,0:T(8,128)(2,1)} %get-tuple-element.6.cols_ref) | copy-start | bytes 6291460
  89.6 1.0 copy-start.1
  90.7 21.3 %copy-start.3 = (bf16[4,32,8,256]{3,2,1,0:T(8,128)(2,1)S(1)}, bf16[4,32,8,256]{3,2,1,0:T(8,128)(2,1)}, u32[]{:S(2)}) copy-start(bf16[4,32,8,256]{3,2,1,0:T(8,128)(2,1)} %get-tuple-element.7) | copy-start | bytes 1572868

commit v4 on v3

--- a/solution.py
+++ b/solution.py
@@ -319,19 +319,21 @@
         for copy in copies:
             copy.wait_recv()
 
-    def run(stages):
+    def run(stages, lead):
         flying = [[None] * chunks for _ in stages]
-        for step in range(chunks + len(stages) - 1):
-            for level in range(len(stages) - 1, -1, -1):
-                c = step - level
-                if 0 <= c < chunks:
-                    if level:
-                        wait(flying[level - 1][c])
-                    flying[level][c] = stages[level](c)
+        order = sorted(
+            (c + sum(lead[:level]), -level, level, c)
+            for level in range(len(stages))
+            for c in range(chunks)
+        )
+        for _, _, level, c in order:
+            if level:
+                wait(flying[level - 1][c])
+            flying[level][c] = stages[level](c)
         for c in range(chunks):
             wait(flying[-1][c])
 
-    run([core_start, row_start, z_start, sub_start])
+    run([core_start, row_start, z_start, sub_start], [1, chunks - 1, chunks - 1])
 
     tiles = vis_ref.shape[0]
 
@@ -373,7 +375,7 @@
         mine = g_ref.at[c, :, core]
         return [send_to(1, c, 0, mine, mine, other)]
 
-    run([back_sub, back_z, back_row, back_core])
+    run([back_sub, back_z, back_row, back_core], [chunks - 1, 2, 3])
 
     total_ref[...] = jnp.zeros_like(total_ref)
 
@@ -450,31 +452,31 @@
     )
 
 
-def spread_kernel(strip_ref, cols_ref, out_ref):
-    pixels = cols_ref.shape[0]
-    block = 1024
-
-    @pl.loop(0, pixels // block)
+def spread_kernel(strip_ref, cols_ref, out_ref, turned_ref):
+    turned_ref[...] = cols_ref[...].astype(F32).T.astype(BF16)
+    count = strip_ref.shape[0]
+    block = math.gcd(count, 256)
+
+    @pl.loop(0, count // block)
     def _(i):
         at = pl.ds(pl.multiple_of(i * block, block), block)
-        out_ref[:, at] = lax.dot_general(
-            strip_ref[...], cols_ref[at], (((1,), (1,)), ((), ())), preferred_element_type=F32
-        ).astype(BF16)
+        out_ref[at] = dot(strip_ref[at], turned_ref[...]).astype(BF16)
 
 
 def spread(strips, columns):
     count, lanes = strips.shape
     pixels = columns.shape[0]
-    tile = math.gcd(count, 256)
+    block = math.gcd(pixels, 1024)
     return pl.pallas_call(
         spread_kernel,
-        grid=(count // tile,),
+        grid=(pixels // block,),
         out_shape=jax.ShapeDtypeStruct((count, pixels), BF16),
         in_specs=[
-            pl.BlockSpec((tile, lanes), lambda i: (i, 0)),
-            pl.BlockSpec((pixels, lanes), lambda i: (0, 0)),
+            pl.BlockSpec((count, lanes), lambda i: (0, 0)),
+            pl.BlockSpec((block, lanes), lambda i: (i, 0)),
         ],
-        out_specs=pl.BlockSpec((tile, pixels), lambda i: (i, 0)),
+        out_specs=pl.BlockSpec((count, block), lambda i: (0, i)),
+        scratch_shapes=[pltpu.VMEM((lanes, block), BF16)],
         compiler_params=pltpu.CompilerParams(vmem_limit_bytes=32 * 2**20),
     )(strips, columns)
 

time: 114 us -> 113 us (level)
    pallas_call x1, Pallas kernels: 82.5 us -> 81.4 us  [exchange(): pl.pallas_call(functools.partial(cycle_kernel, pixels), out_shape=(jax.Sh...]
where the time goes in v4:
time: 113 us; the launch traced here: 112 us
  Pallas kernels  103 us (91%)
  local copies, waits for them, and re-layouts  5.61 us (5%)
  other arithmetic  1.95 us (2%)
  between operations  1.36 us (1%)
    pallas_call x1, Pallas kernels, exchange(): pl.pallas_call(functools.partial(cycle_kernel, pixels), out_shape=(jax.Sh...  81.4 us
    pallas_call x1, Pallas kernels, spread(): pl.pallas_call(spread_kernel, grid=(pixels // block,), out_shape=jax.Shap...  21.3 us
    unnamed x9, local copies, waits for them, and re-layouts  3.43 us

profile of v4, /device:TPU:0, one launch (start us, length us, event | category | flops | bytes accessed | tf_op | source)
XLA Modules:
  0.0 111.6 jit_solution(7564304581360705901)
XLA Ops:
  1.3 0.1 add.96
  1.4 1.3 %copy.12.list_ref = s32[32,1]{1,0:T(8,128)} copy(s32[32,1]{0,1:T(1,128)} %bitcast.20) | data formatting | bytes 256 | tf_op jit(solution)/shard_map/reshape | solution.py:450
  2.7 0.3 fusion.18
  3.0 0.3 multiply_convert_fusion
  3.5 0.0 copy-start.2
  3.5 0.6 multiply_convert_fusion.3
  4.1 0.7 pad_maximum_fusion.1
  4.7 0.8 copy.11
  5.5 0.0 copy-done.2
  5.5 81.4 %shard_map.68 = (bf16[4,512,128]{2,1,0:T(8,128)(2,1)}, bf16[4,32,8,256]{3,2,1,0:T(8,128)(2,1)}, bf16[8192,128]{1,0:T(8,128)(2,1)}) custom-call(s32[32]{0:T(128)} %offset_ref.1, s32[1]{0:T(128)S(6)} %copy.14.count_ref, s32[1,4]{1,0:T(1,128)} %place_ref.1, s32[32,1]{1,0:T(8,128)} %copy.12.list_ref, bf16[2048,8192]{1,0:T(8,128)(2,1)} %bitcast.13, ...), custom_call_target="tpu_custom_call" | custom-call | tf_op jit(solution)/shard_map/pallas_call | solution.py:413
  86.8 0.0 copy-start
  86.9 1.6 %copy-done = bf16[8192,128]{1,0:T(8,128)(2,1)S(1)} copy-done((bf16[8192,128]{1,0:T(8,128)(2,1)S(1)}, bf16[8192,128]{1,0:T(8,128)(2,1)}, u32[]{:S(2)}) %copy-start) | copy-done | bytes 2097176
  88.4 0.0 copy-start.1
  88.4 1.0 copy-done.1
  89.5 0.0 copy-start.3
  89.5 21.3 %shard_map.69 = bf16[2048,8192]{1,0:T(8,128)(2,1)} custom-call(bf16[2048,128]{1,0:T(8,128)(2,1)S(1)} %bitcast.12, bf16[8192,128]{1,0:T(8,128)(2,1)S(1)} %copy-done), custom_call_target="tpu_custom_call" | custom-call | tf_op jit(solution)/shard_map/pallas_call | solution.py:470
  110.8 0.0 copy-done.3
  110.8 0.8 copy.15
  (5 shorter events, 0.1 us)
Async XLA Ops:
  3.5 2.0 %copy-start.2 = (bf16[2,2,64,256]{3,2,1,0:T(8,128)(2,1)}, bf16[2,2,64,256]{3,2,1,0:T(8,128)(2,1)S(1)}, u32[]{:S(2)}) copy-start(bf16[2,2,64,256]{3,2,1,0:T(8,128)(2,1)S(1)} %copy.10) | copy-start | bytes 393220
  86.8 1.6 %copy-start = (bf16[8192,128]{1,0:T(8,128)(2,1)S(1)}, bf16[8192,128]{1,0:T(8,128)(2,1)}, u32[]{:S(2)}) copy-start(bf16[8192,128]{1,0:T(8,128)(2,1)} %get-tuple-element.6.cols_ref) | copy-start | bytes 6291460
  88.4 1.0 copy-start.1
  89.5 21.3 %copy-start.3 = (bf16[4,32,8,256]{3,2,1,0:T(8,128)(2,1)S(1)}, bf16[4,32,8,256]{3,2,1,0:T(8,128)(2,1)}, u32[]{:S(2)}) copy-start(bf16[4,32,8,256]{3,2,1,0:T(8,128)(2,1)} %get-tuple-element.7) | copy-start | bytes 1572868
